TPU v7x, 256 devices: a whole 4x4x8 slice. The times are simulated.
256 devices in a mesh: fsdp: 32 (over y, x, core), tp: 8 (over z).
Axes of the slice: x: 4, y: 4, z: 8, core: 2. Of those that a mesh axis runs over, the one named last changes fastest.
Arguments:
- grad: bfloat16 [8192, 28672], P('fsdp', 'tp'), may hold values from -54 to 54, as said below
- momentum: bfloat16 [8192, 28672], P('fsdp', 'tp'), may hold values from -6 to 6
- basis: bfloat16 [28672, 256], P('tp'), may hold values from -6 to 6
Outputs:
- update: bfloat16 [8192, 28672], P('fsdp', 'tp')
- new_momentum: bfloat16 [8192, 28672], P('fsdp', 'tp')
- new_basis: bfloat16 [28672, 256], P('tp')
Inputs may be any that keep to these rules, and one draw needn't show every extreme that they name: `grad`: a gradient whose rows and columns carry scales of about 0.3 to 3.
All inputs are finite; a program needn't handle non-finite values.
Results may differ from a plain program's by a relative error of at most 0.0078.
Values may be sent and summed in bfloat16 or wider, within the bound.
A program may use at most 64 MiB of HBM per device.

v0:
```python
import math

import jax
import jax.numpy as jnp
from jax import lax
from jax.sharding import PartitionSpec as P

M = 8192
N = 28672
RANK = 256
MU = 90


def orthonormal(left, gram):
    lower = jnp.linalg.cholesky(gram)
    return lax.linalg.triangular_solve(
        lower, left, left_side=False, lower=True, transpose_a=True
    ).astype(jnp.bfloat16)


def gram_of(left):
    return jnp.dot(
        left.T, left, precision=lax.Precision.HIGHEST, preferred_element_type=jnp.float32
    )


def body(grad, momentum, basis):
    buffer = momentum.astype(jnp.float32) + grad.astype(jnp.float32)
    buffer_half = buffer.astype(jnp.bfloat16)
    partial_left = jnp.dot(buffer_half, basis, preferred_element_type=jnp.float32) * (
        1.0 / math.sqrt(N)
    )
    left = lax.psum(partial_left, "tp")
    gram = lax.psum(gram_of(left), "fsdp")
    ortho = orthonormal(left, gram)
    partial_right = lax.dot_general(
        buffer_half, ortho, (((0,), (0,)), ((), ())), preferred_element_type=jnp.float32
    )
    right = lax.psum(partial_right, "fsdp")
    squares = lax.psum(jnp.sum(right * right, axis=0), "tp")
    scale = jnp.sqrt(squares / N + 1e-06)
    new_basis = (right / scale[None, :]).astype(jnp.bfloat16)
    scaled = (ortho.astype(jnp.float32) * scale[None, :]).astype(jnp.bfloat16)
    lowrank = lax.dot_general(
        scaled, new_basis, (((1,), (1,)), ((), ())), preferred_element_type=jnp.float32
    )
    new_momentum = (buffer - (1.0 - MU / 100.0) * lowrank).astype(jnp.bfloat16)
    product = lax.dot_general(
        ortho, new_basis, (((1,), (1,)), ((), ())), preferred_element_type=jnp.float32
    )
    update = (product * math.sqrt(M / RANK)).astype(jnp.bfloat16)
    return (update, new_momentum, new_basis)


def solution(mesh):
    placed = (P("fsdp", "tp"), P("fsdp", "tp"), P("tp", None))
    return jax.shard_map(
        body,
        mesh=mesh,
        in_specs=placed,
        out_specs=(P("fsdp", "tp"), P("fsdp", "tp"), P("tp", None)),
        check_vma=False,
    )
```

profile of v0, /device:TPU:1, one launch (start us, length us, event | category | flops | bytes accessed | tf_op | source)
XLA Modules:
  0.0 420.6 jit_solution(16126735888261993568)
XLA Ops:
  7.2 1.4 copy-done
  8.7 3.4 convolution_multiply_fusion.2
  12.1 71.9 %all-reduce.5.cloned.1.call-done = f32[256,256]{1,0:T(8,128)} async-done(((f32[256,256]{1,0:T(8,128)}), f32[256,256]{1,0:T(8,128)}) %all-reduce.5.cloned.1.call-update) | async-done | bytes 262160 | tf_op jit(solution)/shard_map/psum | solution.py:33
  84.0 2.3 fusion.20
  86.4 116.0 %all-reduce.7.cloned.1.call-done = f32[256,256]{0,1:T(8,128)} async-done(((f32[256,256]{0,1:T(8,128)}), f32[256,256]{0,1:T(8,128)}) %all-reduce.7.cloned.1.call-update) | async-done | bytes 262160 | tf_op jit(solution)/shard_map/psum | solution.py:34
  202.4 1.1 copy.7
  203.5 1.0 fusion.7
  204.6 11.7 %cholesky.50 = f32[128,128]{1,0:T(8,128)S(1)} custom-call(f32[128,128]{1,0:T(8,128)S(1)} %cholesky.118), custom_call_target="Cholesky" | custom-call | tf_op jit(solution)/shard_map/jit(cholesky)/cholesky | solution.py:15
  216.3 9.8 %custom-call.14 = f32[1,128,128]{1,2,0:T(8,128)S(1)} custom-call(f32[1,128,128]{2,1,0:T(8,128)S(1)} %get-tuple-element.24), custom_call_target="InvertDiagBlocksLowerTriangular" | custom-call | tf_op jit(solution)/shard_map/jit(cholesky)/cholesky | solution.py:15
  226.6 11.7 %cholesky.105 = f32[128,128]{1,0:T(8,128)S(1)} custom-call(f32[128,128]{1,0:T(8,128)S(1)} %convolution_subtract_fusion.1), custom_call_target="Cholesky" | custom-call | tf_op jit(solution)/shard_map/jit(cholesky)/cholesky | solution.py:15
  238.4 0.6 compare_reduce_fusion
  240.4 4.1 while.1
  240.6 0.6 fusion.31
  241.2 1.4 bitcast_dynamic-update-slice_fusion.2
  242.6 0.6 fusion.31
  243.2 1.4 bitcast_dynamic-update-slice_fusion.2
  244.6 19.7 %custom-call.15 = f32[2,128,128]{1,2,0:T(8,128)S(1)} custom-call(f32[2,128,128]{2,1,0:T(8,128)S(1)} %get-tuple-element.10), custom_call_target="InvertDiagBlocksLowerTriangular" | custom-call | tf_op jit(solution)/shard_map/triangular_solve | solution.py:16
  265.3 4.6 %fusion.4 = f32[3584,256]{1,0:T(8,128)} fusion(bf16[256,3584]{1,0:T(8,128)(2,1)} %param.3, bf16[256,3584]{1,0:T(8,128)(2,1)} %param.4, bf16[256,128]{0,1:T(8,128)(2,1)S(1)} %convolution_convert_fusion, bf16[256,128]{0,1:T(8,128)(2,1)S(1)} %get-tuple-element.27), kind=kOutput, calls=%fused_computation.15 | convolution fusion | flops 473694208 | bytes 7471104 | tf_op jit(solution)/shard_map/dot_general | solution.py:36
  269.9 120.6 %all-reduce.9.cloned.1.call-done = f32[3584,256]{1,0:T(8,128)} async-done(((f32[3584,256]{1,0:T(8,128)}), f32[3584,256]{1,0:T(8,128)}) %all-reduce.9.cloned.1.call-update) | async-done | bytes 3670032 | tf_op jit(solution)/shard_map/psum | solution.py:39
  390.5 2.5 multiply_reduce_fusion
  393.1 13.7 %psum.31 = f32[256]{0:T(256)S(1)} all-reduce(f32[256]{0:T(256)S(1)} %multiply_reduce_fusion), channel_id=1, replica_groups=mesh['fsdp'=32,'tp'=8] {'tp'}, use_global_device_ids=true, to_apply=%region_8.9 | all-reduce | flops 256 | bytes 2048 | tf_op jit(solution)/shard_map/psum | solution.py:40
  406.8 2.5 divide_convert_fusion
  409.9 2.2 fusion.2
  412.2 1.9 fusion.1
  (31 shorter events, 2.6 us)
Async XLA Ops:
  7.2 1.5 copy-start
  7.2 76.8 %all-reduce.5.cloned.1.call-start = ((), (), s32[]{:S(2)}) async-start(), calls=%async_computation | async-start | bytes 524288 | tf_op jit(solution)/shard_map/psum | solution.py:33
  12.1 190.3 %all-reduce.7.cloned.1.call-start = ((), (), s32[]{:S(2)}) async-start(), calls=%async_computation.1 | async-start | bytes 524288 | tf_op jit(solution)/shard_map/psum | solution.py:34
  86.4 304.2 %all-reduce.9.cloned.1.call-start = ((), (), s32[]{:S(2)}) async-start(), calls=%async_computation.2 | async-start | bytes 7340032 | tf_op jit(solution)/shard_map/psum | solution.py:39
  203.5 60.8 %copy-start.4 = (f32[256,256]{1,0:T(8,128)S(1)}, f32[256,256]{1,0:T(8,128)}, u32[]{:S(2)}) copy-start(f32[256,256]{1,0:T(8,128)} %all-reduce.5.cloned.1.call-done) | copy-start | bytes 786436
  406.8 2.6 copy-start.1
  406.8 3.2 copy-start.2
  409.9 2.2 copy-start.3
Sparse Core Ops, SparseCore 0:
  12.2 71.7 all-reduce.4
  88.1 114.2 all-reduce.6
  270.0 120.4 all-reduce.8
where the time goes:
time: 425 us; the launch traced here: 421 us
  waiting for transfers between devices  309 us (73%)
  other arithmetic  59.7 us (14%)
  matrix products  16 us (4%)
  between operations  15.2 us (4%)
  blocking collectives  13.7 us (3%)
  local copies, waits for them, and re-layouts  7.23 us (2%)
    psum x1, waiting for transfers between devices, body(): right = lax.psum(partial_right, 'fsdp')  121 us
    psum x1, waiting for transfers between devices, body(): gram = lax.psum(gram_of(left), 'fsdp')  116 us
    psum x1, waiting for transfers between devices, body(): left = lax.psum(partial_left, 'tp')  71.9 us
    another operation x6, other arithmetic, orthonormal(): lower = jnp.linalg.cholesky(gram)  34 us
    another operation x3, other arithmetic, orthonormal(): lax.linalg.triangular_solve(lower, left, left_side=False, lower=True, tra...  19.7 us
    psum x1, blocking collectives, body(): squares = lax.psum(jnp.sum(right * right, axis=0), 'tp')  13.7 us
  transfers between devices with their start and end apart: 3, of which 3 were waited for; matrix products, arithmetic and copies ran while one was open for 0% of the time, Pallas kernels for 0%

commit v1 on v0

v1 whole, which is shorter than its diff:
```python
import math

import jax
import jax.numpy as jnp
from jax import lax
from jax.experimental import pallas as pl
from jax.experimental.pallas import tpu as pltpu
from jax.sharding import PartitionSpec as P

M = 8192
N = 28672
RANK = 256
MU = 90

MESH = pl.DeviceIdType.MESH
HI = lax.Precision.HIGHEST
F32 = jnp.float32
BF16 = jnp.bfloat16
NX, NY, NZ = 4, 4, 8
NF = NX * NY * 2
ROWS = M // NF
COLS = N // NZ
CHUNK = 896
BLOCK = COLS // NF
VMEM_LIMIT = 48 * 1024 * 1024


def dot(a, b, ca, cb, precision=None):
    return lax.dot_general(
        a, b, (((ca,), (cb,)), ((), ())), precision=precision, preferred_element_type=F32
    )


def lower_inverse(gram, b=32, s8=8):
    n = gram.shape[0]
    rows = lax.broadcasted_iota(jnp.int32, (8, 128), 0)
    lanes = lax.broadcasted_iota(jnp.int32, (b, n), 1)
    sub = lax.broadcasted_iota(jnp.int32, (b, n), 0)
    panels = [gram[p * b:(p + 1) * b, :] for p in range(n // b)]
    done = []
    tiles = b // 8
    for p in range(n // b):
        r0 = p * b
        P = panels[p]
        nt = n // 128
        home = r0 // 128
        ident = jnp.where(lanes == sub + r0, 1.0, 0.0)[:, home * 128:(home + 1) * 128]
        M = [[P[8 * a:8 * a + 8, 128 * l:128 * l + 128] for l in range(nt)] + [ident[8 * a:8 * a + 8]] for a in range(tiles)]
        piv = [jnp.ones((8, 128), jnp.float32) for _ in range(tiles)]
        for s in range(b // s8):
            a0 = s
            C = []
            for k in range(s8):
                lane = r0 - home * 128 + s * s8 + k
                C.append([jnp.broadcast_to(M[a][home][:, lane:lane + 1], (8, 128)) if a >= a0 else None for a in range(tiles)])
            for j in range(s8):
                sj = jnp.broadcast_to(C[j][a0][j:j + 1, :], (8, 128))
                inv = 1.0 / sj
                w = [None] * tiles
                for a in range(a0, tiles):
                    wa = C[j][a] * inv
                    if a == a0:
                        wa = jnp.where(rows > j, wa, 0.0)
                    w[a] = wa
                for k in range(j + 1, s8):
                    bk = jnp.broadcast_to(C[j][a0][k:k + 1, :], (8, 128))
                    for a in range(a0, tiles):
                        C[k][a] = C[k][a] - w[a] * bk
                piv[a0] = jnp.where(rows == j, sj, piv[a0])
                for l in range(nt + 1):
                    row = jnp.broadcast_to(M[a0][l][j:j + 1, :], (8, 128))
                    for a in range(a0, tiles):
                        M[a][l] = M[a][l] - w[a] * row
        rs = [lax.rsqrt(v) for v in piv]
        full = []
        for a in range(tiles):
            out = [M[a][l] * rs[a] for l in range(nt + 1)]
            z = out.pop()
            ln = lax.broadcasted_iota(jnp.int32, (8, 128), 1) + home * 128
            out[home] = jnp.where((ln >= r0) & (ln < r0 + b), z, out[home])
            full.append(jnp.concatenate(out, axis=1))
        U = jnp.concatenate(full, axis=0)
        done.append(U)
        if p + 1 < n // b:
            r1 = r0 + b
            upd = lax.dot_general(U, U, (((0,), (0,)), ((), ())), precision=HI, preferred_element_type=jnp.float32)
            for q in range(p + 1, n // b):
                old = jnp.where((lanes >= r0) & (lanes < r1), 0.0, panels[q])
                panels[q] = old - upd[q * b:(q + 1) * b, :]
    W = jnp.concatenate(done, axis=0)
    li = lax.broadcasted_iota(jnp.int32, (n, n), 1)
    si = lax.broadcasted_iota(jnp.int32, (n, n), 0)
    return jnp.where(li <= si, W, 0.0)


def gram_kernel(g_hbm, m_hbm, b_hbm, left, gram, gbuf, mbuf, bbuf, part, rz, gpart, rg, own, r2,
                load, s_rz, r_rz, s_az, r_az, s_rg, r_rg, s_r2, r_r2, s_ag, r_ag):
    f = lax.axis_index("fsdp")
    t = lax.axis_index("tp")
    nc = COLS // CHUNK
    loads = []
    for c in range(nc):
        cols = pl.ds(c * CHUNK, CHUNK)
        three = [
            pltpu.make_async_copy(g_hbm.at[:, cols], gbuf.at[:, cols], load.at[3 * c]),
            pltpu.make_async_copy(m_hbm.at[:, cols], mbuf.at[:, cols], load.at[3 * c + 1]),
            pltpu.make_async_copy(b_hbm.at[cols, :], bbuf.at[cols, :], load.at[3 * c + 2]),
        ]
        for cp in three:
            cp.start()
        loads.append(three)
    zs = [lax.rem(t + j, NZ) for j in range(NZ)]
    fs = [lax.rem(f + j, NF) for j in range(NF)]
    barrier = pltpu.get_barrier_semaphore()
    for j in range(1, NZ):
        pl.semaphore_signal(barrier, inc=1, device_id=(f, zs[j]), device_id_type=MESH)
    for j in range(1, NF):
        pl.semaphore_signal(barrier, inc=1, device_id=(fs[j], t), device_id_type=MESH)

    for c in range(nc):
        for cp in loads[c]:
            cp.wait()
        cols = pl.ds(c * CHUNK, CHUNK)
        half = (mbuf[:, cols].astype(F32) + gbuf[:, cols].astype(F32)).astype(BF16)
        term = dot(half, bbuf[cols, :], 1, 0)
        if c == 0:
            part[...] = term
        else:
            part[...] += term
    part[...] = part[...] * (1.0 / math.sqrt(N))
    pl.semaphore_wait(barrier, NZ - 1 + NF - 1)

    def piece(z, size):
        return pl.ds(pl.multiple_of(z * size, size), size)

    sends = []

    def exchange(j, src, dst, ss, rs, dev):
        cp = pltpu.make_async_remote_copy(
            src_ref=src, dst_ref=dst, send_sem=ss.at[j - 1], recv_sem=rs.at[j - 1],
            device_id=dev, device_id_type=MESH,
        )
        cp.start()
        sends.append(cp)
        return cp

    zr = ROWS // NZ
    cps = [exchange(j, part.at[piece(zs[j], zr), :], rz.at[j - 1], s_rz, r_rz, (f, zs[j])) for j in range(1, NZ)]
    mine = part[piece(t, zr), :]
    for j in range(1, NZ):
        cps[j - 1].wait_recv()
        mine = mine + rz[j - 1]
    left[piece(t, zr), :] = mine
    az = [exchange(j, left.at[piece(t, zr), :], left.at[piece(t, zr), :], s_az, r_az, (f, zs[j])) for j in range(1, NZ)]

    gr = RANK // NF
    gpart[...] = dot(mine, mine, 0, 0, HI)
    cps = [exchange(j, gpart.at[piece(fs[j], gr), :], rg.at[j - 1], s_rg, r_rg, (fs[j], t)) for j in range(1, NF)]
    acc = gpart[piece(f, gr), :]
    for j in range(1, NF):
        cps[j - 1].wait_recv()
        acc = acc + rg[j - 1]
    own[...] = acc
    cps = [exchange(j, own, r2.at[j - 1], s_r2, r_r2, (f, zs[j])) for j in range(1, NZ)]
    for j in range(1, NZ):
        cps[j - 1].wait_recv()
        acc = acc + r2[j - 1]
    gram[piece(f, gr), :] = acc
    cps = [exchange(j, gram.at[piece(f, gr), :], gram.at[piece(f, gr), :], s_ag, r_ag, (fs[j], t)) for j in range(1, NF)]
    for cp in cps:
        cp.wait_recv()
    for cp in az:
        cp.wait_recv()
    for cp in sends:
        cp.wait_send()


def factor_kernel(gram, left, inverse, ortho):
    w = lower_inverse(gram[...])
    inverse[...] = w
    ortho[...] = dot(left[...], w, 1, 1, HI).astype(BF16)


def right_kernel(g_hbm, m_hbm, left, inverse, out, squares, gbuf, mbuf, r, rc, ra, rb, sa, sb, ra2, rb2, sq, sz,
                 load, s_c, r_c, s_1, r_1, s_2, r_2, s_q, r_q, s_z, r_z, s_g2, r_g2, s_g1, r_g1, s_gc, r_gc):
    f = lax.axis_index("fsdp")
    t = lax.axis_index("tp")
    core = lax.rem(f, 2)
    x = lax.rem(f // 2, NX)
    y = f // (2 * NX)
    other = 1 - core

    def dev(px, py, pc):
        return ((py * NX + px) * 2 + pc, t)

    xs = [lax.rem(x + j, NX) for j in range(NX)]
    ys = [lax.rem(y + j, NY) for j in range(NY)]
    zs = [lax.rem(t + j, NZ) for j in range(NZ)]
    fs = [lax.rem(f + j, NF) for j in range(NF)]
    sibling = dev(x, y, other)
    wide = COLS // 2
    nk = wide // CHUNK
    qk = NX // nk
    loads = []
    for i, pc in enumerate((other, core)):
        for k in range(nk):
            cols = pl.ds(pl.multiple_of(pc * wide + k * CHUNK, 128), CHUNK)
            two = [
                pltpu.make_async_copy(g_hbm.at[:, cols], gbuf.at[:, cols], load.at[2 * (i * nk + k)]),
                pltpu.make_async_copy(m_hbm.at[:, cols], mbuf.at[:, cols], load.at[2 * (i * nk + k) + 1]),
            ]
            for cp in two:
                cp.start()
            loads.append((cols, two))
    barrier = pltpu.get_barrier_semaphore()
    for j in range(1, NZ):
        pl.semaphore_signal(barrier, inc=1, device_id=(f, zs[j]), device_id_type=MESH)
    for j in range(1, NF):
        pl.semaphore_signal(barrier, inc=1, device_id=(fs[j], t), device_id_type=MESH)

    sends = []

    def exchange(src, dst, ss, rs, device):
        cp = pltpu.make_async_remote_copy(
            src_ref=src, dst_ref=dst, send_sem=ss, recv_sem=rs, device_id=device, device_id_type=MESH
        )
        cp.start()
        sends.append(cp)
        return cp

    hi = left[...].astype(BF16)
    lo = (left[...] - hi.astype(F32)).astype(BF16)

    def product(i, k, pc):
        cols, two = loads[i * nk + k]
        for cp in two:
            cp.wait()
        half = (mbuf[:, cols].astype(F32) + gbuf[:, cols].astype(F32)).astype(BF16)
        val = dot(half, hi, 0, 0) + dot(half, lo, 0, 0)
        for h in range(2):
            r[h, pc, k * qk:(k + 1) * qk] = val[:, 128 * h:128 * h + 128].reshape(qk, NY, BLOCK, 128)

    cc = []
    for k in range(nk):
        product(0, k, other)
        if k == 0:
            pl.semaphore_wait(barrier, NZ - 1 + NF - 1)
        qs = pl.ds(k * qk, qk)
        cc.append([
            exchange(r.at[h, other, qs], rc.at[h, qs], s_c.at[2 * k + h], r_c.at[2 * k + h], sibling)
            for h in range(2)
        ])
    for k in range(nk):
        product(1, k, core)
    for k in range(nk):
        for h in range(2):
            cc[k][h].wait_recv()
            qs = pl.ds(k * qk, qk)
            r[h, core, qs] = r[h, core, qs] + rc[h, qs]
    one = []
    for j in range(1, NX):
        one.append(exchange(r.at[0, core, xs[j]], ra.at[j - 1], s_1.at[j - 1], r_1.at[j - 1], dev(xs[j], y, core)))
        one.append(exchange(r.at[1, core, :, ys[j]], rb.at[j - 1], s_1.at[2 + j], r_1.at[2 + j], dev(x, ys[j], core)))
    for cp in one:
        cp.wait_recv()
    sa[...] = r[0, core, x] + ra[0] + ra[1] + ra[2]
    sb[...] = r[1, core, :, y] + rb[0] + rb[1] + rb[2]
    two = []
    for j in range(1, NX):
        two.append(exchange(sa.at[ys[j]], ra2.at[j - 1], s_2.at[j - 1], r_2.at[j - 1], dev(x, ys[j], core)))
        two.append(exchange(sb.at[xs[j]], rb2.at[j - 1], s_2.at[2 + j], r_2.at[2 + j], dev(xs[j], y, core)))
    for cp in two:
        cp.wait_recv()
    shard = jnp.concatenate(
        [sa[y] + ra2[0] + ra2[1] + ra2[2], sb[x] + rb2[0] + rb2[1] + rb2[2]], axis=1
    )
    right = dot(shard, inverse[...], 1, 1, HI)
    sq[f] = jnp.broadcast_to(jnp.sum(right * right, axis=0, keepdims=True), (8, RANK))
    sqs = [exchange(sq.at[f], sq.at[f], s_q.at[j - 1], r_q.at[j - 1], (fs[j], t)) for j in range(1, NF)]
    rounded = right.astype(BF16)
    for h in range(2):
        out[h, core, x, y] = rounded[:, 128 * h:128 * h + 128]
    g2 = []
    for j in range(1, NX):
        g2.append(exchange(out.at[0, core, x, y], out.at[0, core, x, y], s_g2.at[j - 1], r_g2.at[j - 1], dev(x, ys[j], core)))
        g2.append(exchange(out.at[1, core, x, y], out.at[1, core, x, y], s_g2.at[2 + j], r_g2.at[2 + j], dev(xs[j], y, core)))
    for cp in g2:
        cp.wait_recv()
    g1 = []
    for j in range(1, NX):
        g1.append(exchange(out.at[0, core, x], out.at[0, core, x], s_g1.at[j - 1], r_g1.at[j - 1], dev(xs[j], y, core)))
        g1.append(exchange(out.at[1, core, :, y], out.at[1, core, :, y], s_g1.at[2 + j], r_g1.at[2 + j], dev(x, ys[j], core)))
    gc = [
        exchange(out.at[0, core, x], out.at[0, core, x], s_gc.at[0], r_gc.at[0], sibling),
        exchange(out.at[1, core, :, y], out.at[1, core, :, y], s_gc.at[1], r_gc.at[1], sibling),
    ]
    for cp in sqs:
        cp.wait_recv()
    sz[t] = jnp.sum(sq[...], axis=0)
    szs = [exchange(sz.at[t], sz.at[t], s_z.at[j - 1], r_z.at[j - 1], (f, zs[j])) for j in range(1, NZ)]
    for j in range(1, NX):
        g1[2 * j - 2].wait_recv()
        px = lax.rem(x + NX - j, NX)
        gc.append(exchange(out.at[0, core, px], out.at[0, core, px], s_gc.at[2 * j], r_gc.at[2 * j], sibling))
        g1[2 * j - 1].wait_recv()
        py = lax.rem(y + NY - j, NY)
        gc.append(exchange(out.at[1, core, :, py], out.at[1, core, :, py], s_gc.at[2 * j + 1], r_gc.at[2 * j + 1], sibling))
    for cp in szs:
        cp.wait_recv()
    squares[...] = jnp.sum(sz[...], axis=0)
    for cp in gc:
        cp.wait_recv()
    for cp in sends:
        cp.wait_send()


def output_kernel(g, m, ortho, right, squares, update, new_momentum, new_basis):
    scale = jnp.sqrt(squares[0:1, :] / N + 1e-06)
    rr = jnp.concatenate([right[0], right[1]], axis=1).astype(F32)
    nb = (rr / scale).astype(BF16)
    new_basis[...] = nb
    scaled = (ortho[...].astype(F32) * scale).astype(BF16)
    lowrank = dot(scaled, nb, 1, 1)
    buffer = m[...].astype(F32) + g[...].astype(F32)
    new_momentum[...] = (buffer - (1.0 - MU / 100.0) * lowrank).astype(BF16)
    update[...] = (dot(ortho[...], nb, 1, 1) * math.sqrt(M / RANK)).astype(BF16)


def body(grad, momentum, basis):
    anywhere = pl.BlockSpec(memory_space=pl.ANY)
    vmem = pl.BlockSpec(memory_space=pltpu.VMEM)
    dma = pltpu.SemaphoreType.DMA
    zr, gr = ROWS // NZ, RANK // NF
    left, gram = pl.pallas_call(
        gram_kernel,
        out_shape=(jax.ShapeDtypeStruct((ROWS, RANK), F32), jax.ShapeDtypeStruct((RANK, RANK), F32)),
        in_specs=[anywhere] * 3,
        out_specs=(vmem, vmem),
        scratch_shapes=[
            pltpu.VMEM((ROWS, COLS), BF16), pltpu.VMEM((ROWS, COLS), BF16), pltpu.VMEM((COLS, RANK), BF16),
            pltpu.VMEM((ROWS, RANK), F32), pltpu.VMEM((NZ - 1, zr, RANK), F32),
            pltpu.VMEM((RANK, RANK), F32), pltpu.VMEM((NF - 1, gr, RANK), F32),
            pltpu.VMEM((gr, RANK), F32), pltpu.VMEM((NZ - 1, gr, RANK), F32),
            dma((3 * (COLS // CHUNK),)),
            dma((NZ - 1,)), dma((NZ - 1,)), dma((NZ - 1,)), dma((NZ - 1,)),
            dma((NF - 1,)), dma((NF - 1,)), dma((NZ - 1,)), dma((NZ - 1,)), dma((NF - 1,)), dma((NF - 1,)),
        ],
        compiler_params=pltpu.CompilerParams(collective_id=0, has_side_effects=True, vmem_limit_bytes=VMEM_LIMIT),
        name="gram_kernel",
    )(grad, momentum, basis)
    inverse, ortho = pl.pallas_call(
        factor_kernel,
        out_shape=(jax.ShapeDtypeStruct((RANK, RANK), F32), jax.ShapeDtypeStruct((ROWS, RANK), BF16)),
        in_specs=[vmem, vmem],
        out_specs=(vmem, vmem),
        compiler_params=pltpu.CompilerParams(vmem_limit_bytes=VMEM_LIMIT),
        name="factor_kernel",
    )(gram, left)
    right, squares = pl.pallas_call(
        right_kernel,
        out_shape=(
            jax.ShapeDtypeStruct((2, 2, NX, NY, BLOCK, 128), BF16),
            jax.ShapeDtypeStruct((8, RANK), F32),
        ),
        in_specs=[anywhere, anywhere, vmem, vmem],
        out_specs=(vmem, vmem),
        scratch_shapes=[
            pltpu.VMEM((ROWS, COLS), BF16), pltpu.VMEM((ROWS, COLS), BF16),
            pltpu.VMEM((2, 2, NX, NY, BLOCK, 128), F32), pltpu.VMEM((2, NX, NY, BLOCK, 128), F32),
            pltpu.VMEM((NX - 1, NY, BLOCK, 128), F32), pltpu.VMEM((NY - 1, NX, BLOCK, 128), F32),
            pltpu.VMEM((NY, BLOCK, 128), F32), pltpu.VMEM((NX, BLOCK, 128), F32),
            pltpu.VMEM((NY - 1, BLOCK, 128), F32), pltpu.VMEM((NX - 1, BLOCK, 128), F32),
            pltpu.VMEM((NF, 8, RANK), F32), pltpu.VMEM((NZ, 8, RANK), F32),
            dma((2 * (COLS // CHUNK),)),
            dma((4,)), dma((4,)), dma((6,)), dma((6,)), dma((6,)), dma((6,)),
            dma((NF - 1,)), dma((NF - 1,)), dma((NZ - 1,)), dma((NZ - 1,)),
            dma((6,)), dma((6,)), dma((6,)), dma((6,)), dma((8,)), dma((8,)),
        ],
        compiler_params=pltpu.CompilerParams(collective_id=1, has_side_effects=True, vmem_limit_bytes=VMEM_LIMIT),
        name="right_kernel",
    )(grad, momentum, left, inverse)
    step = 512
    return pl.pallas_call(
        output_kernel,
        grid=(COLS // step,),
        out_shape=(
            jax.ShapeDtypeStruct((ROWS, COLS), BF16),
            jax.ShapeDtypeStruct((ROWS, COLS), BF16),
            jax.ShapeDtypeStruct((COLS, RANK), BF16),
        ),
        in_specs=[
            pl.BlockSpec((ROWS, step), lambda i: (0, i)),
            pl.BlockSpec((ROWS, step), lambda i: (0, i)),
            pl.BlockSpec((ROWS, RANK), lambda i: (0, 0)),
            pl.BlockSpec((2, step, 128), lambda i: (0, i, 0)),
            pl.BlockSpec((8, RANK), lambda i: (0, 0)),
        ],
        out_specs=(
            pl.BlockSpec((ROWS, step), lambda i: (0, i)),
            pl.BlockSpec((ROWS, step), lambda i: (0, i)),
            pl.BlockSpec((step, RANK), lambda i: (i, 0)),
        ),
        compiler_params=pltpu.CompilerParams(vmem_limit_bytes=VMEM_LIMIT),
        name="output_kernel",
    )(grad, momentum, ortho, right.reshape(2, COLS, 128), squares)


def solution(mesh):
    placed = (P("fsdp", "tp"), P("fsdp", "tp"), P("tp", None))
    return jax.shard_map(
        body,
        mesh=mesh,
        in_specs=placed,
        out_specs=(P("fsdp", "tp"), P("fsdp", "tp"), P("tp", None)),
        check_vma=False,
    )
```

time: 425 us -> 104 us (0.24)
  waiting for transfers between devices: 309 us -> 0 us
  Pallas kernels: 0 us -> 98.4 us
  other arithmetic: 59.7 us -> 0 us
  matrix products: 16 us -> 0 us
  between operations: 15.2 us -> 0.67 us
  blocking collectives: 13.7 us -> 0 us
    psum x3 -> x0, waiting for transfers between devices: 308 us -> none  [the longest x1 121 us: body(): right = lax.psum(partial_right, 'fsdp')]
    pallas_call x0 -> x4, Pallas kernels: none -> 98.4 us  [the longest x1 43.3 us: body(): pl.pallas_call(right_kernel, out_shape=(jax.ShapeDtypeStruct((2, 2, NX, N...]
    another operation x9 -> x0, other arithmetic: 53.7 us -> none  [the longest x6 34 us: orthonormal(): lower = jnp.linalg.cholesky(gram)]
    dot_general x5 -> x0, matrix products: 14.5 us -> none  [the longest x1 4.58 us: body(): lax.dot_general(buffer_half, ortho, (((0,), (0,)), ((), ())), preferred_e...]
    psum x1 -> x0, blocking collectives: 13.7 us -> none  [body(): squares = lax.psum(jnp.sum(right * right, axis=0), 'tp')]
  transfers between devices with their start and end apart: 3 -> 0, of which waited for: 3 -> 0; matrix products, arithmetic and copies ran while one was open for 0% -> 0% of each run, Pallas kernels for 0% -> 0%
where the time goes in v1:
time: 104 us
  Pallas kernels  98.4 us (95%)
  local copies, waits for them, and re-layouts  4.49 us (4%)
    pallas_call x1, Pallas kernels, body(): pl.pallas_call(right_kernel, out_shape=(jax.ShapeDtypeStruct((2, 2, NX, N...  43.3 us
    pallas_call x1, Pallas kernels, body(): pl.pallas_call(gram_kernel, out_shape=(jax.ShapeDtypeStruct((ROWS, RANK),...  39.4 us
    pallas_call x1, Pallas kernels, body(): pl.pallas_call(factor_kernel, out_shape=(jax.ShapeDtypeStruct((RANK, RANK...  10.7 us
    pallas_call x1, Pallas kernels, body(): pl.pallas_call(output_kernel, grid=(COLS // step,), out_shape=(jax.ShapeD...  4.91 us
    unnamed x8, local copies, waits for them, and re-layouts  4.49 us

profile of v1, /device:TPU:1, one launch (start us, length us, event | category | flops | bytes accessed | tf_op | source)
XLA Modules:
  0.0 103.5 jit_solution(18093632000064310122)
XLA Ops:
  0.6 0.0 copy-start
  0.6 1.5 %copy-done = bf16[256,3584]{1,0:T(8,128)(2,1)S(1)} copy-done((bf16[256,3584]{1,0:T(8,128)(2,1)S(1)}, bf16[256,3584]{1,0:T(8,128)(2,1)}, u32[]{:S(2)}) %copy-start) | copy-done | bytes 1835032
  2.1 0.0 copy-start.2
  2.1 1.5 %copy-done.2 = bf16[256,3584]{1,0:T(8,128)(2,1)S(1)} copy-done((bf16[256,3584]{1,0:T(8,128)(2,1)S(1)}, bf16[256,3584]{1,0:T(8,128)(2,1)}, u32[]{:S(2)}) %copy-start.2) | copy-done | bytes 1835032
  3.6 0.0 copy-start.3
  3.6 1.5 %copy-done.3 = bf16[3584,256]{1,0:T(8,128)(2,1)S(1)} copy-done((bf16[3584,256]{1,0:T(8,128)(2,1)S(1)}, bf16[3584,256]{1,0:T(8,128)(2,1)}, u32[]{:S(2)}) %copy-start.3) | copy-done | bytes 1835032
  5.1 0.0 copy-start.1
  5.1 39.4 %gram_kernel.1 = (f32[256,256]{1,0:T(8,128)S(1)}, f32[256,256]{1,0:T(8,128)S(1)}) custom-call(bf16[256,3584]{1,0:T(8,128)(2,1)S(1)} %copy-done, bf16[256,3584]{1,0:T(8,128)(2,1)S(1)} %copy-done.2, bf16[3584,256]{1,0:T(8,128)(2,1)S(1)} %copy-done.3), custom_call_target="tpu_custom_call" | custom-call | tf_op jit(solution)/shard_map/gram_kernel/pallas_call | solution.py:334
  44.6 10.7 %factor_kernel.1 = (f32[256,256]{1,0:T(8,128)S(1)}, bf16[256,256]{1,0:T(8,128)(2,1)S(1)}) custom-call(f32[256,256]{1,0:T(8,128)S(1)} %get-tuple-element.9.gram, f32[256,256]{1,0:T(8,128)S(1)} %get-tuple-element.10.left), custom_call_target="tpu_custom_call" | custom-call | tf_op jit(solution)/shard_map/factor_kernel/pallas_call | solution.py:351
  55.3 0.0 copy-done.1
  55.3 43.3 %right_kernel.1 = (bf16[2,2,4,4,112,128]{5,4,3,2,1,0:T(8,128)(2,1)S(1)}, f32[8,256]{1,0:T(8,128)S(1)}) custom-call(bf16[256,3584]{1,0:T(8,128)(2,1)S(1)} %copy-done.1, bf16[256,3584]{1,0:T(8,128)(2,1)S(1)} %copy-done.2, f32[256,256]{1,0:T(8,128)S(1)} %get-tuple-element.10.left, f32[256,256]{1,0:T(8,128)S(1)} %get-tuple-element.12.inverse), custom_call_target="tpu_custom_call" | custom-call | tf_op jit(solution)/shard_map/right_kernel/pallas_call | solution.py:359
  98.6 4.9 %output_kernel.1 = (bf16[256,3584]{1,0:T(8,128)(2,1)}, bf16[256,3584]{1,0:T(8,128)(2,1)}, bf16[3584,256]{1,0:T(8,128)(2,1)}) custom-call(bf16[256,3584]{1,0:T(8,128)(2,1)S(1)} %copy-done.1, bf16[256,3584]{1,0:T(8,128)(2,1)S(1)} %copy-done.2, bf16[256,256]{1,0:T(8,128)(2,1)S(1)} %get-tuple-element.11.ortho, bf16[2,3584,128]{2,1,0:T(8,128)(2,1)S(1)} %bitcast.1, ...), custom_call_target="tpu_custom_call" | custom-call | tf_op jit(solution)/shard_map/output_kernel/pallas_call | solution.py:383
Async XLA Ops:
  0.6 1.5 %copy-start = (bf16[256,3584]{1,0:T(8,128)(2,1)S(1)}, bf16[256,3584]{1,0:T(8,128)(2,1)}, u32[]{:S(2)}) copy-start(bf16[256,3584]{1,0:T(8,128)(2,1)} %g.1) | copy-start | bytes 5505028
  2.1 1.5 %copy-start.2 = (bf16[256,3584]{1,0:T(8,128)(2,1)S(1)}, bf16[256,3584]{1,0:T(8,128)(2,1)}, u32[]{:S(2)}) copy-start(bf16[256,3584]{1,0:T(8,128)(2,1)} %m.1) | copy-start | bytes 5505028
  3.6 1.5 %copy-start.3 = (bf16[3584,256]{1,0:T(8,128)(2,1)S(1)}, bf16[3584,256]{1,0:T(8,128)(2,1)}, u32[]{:S(2)}) copy-start(bf16[3584,256]{1,0:T(8,128)(2,1)} %b_hbm.1) | copy-start | bytes 5505028
  5.1 50.1 %copy-start.1 = (bf16[256,3584]{1,0:T(8,128)(2,1)S(1)}, bf16[256,3584]{1,0:T(8,128)(2,1)}, u32[]{:S(2)}) copy-start(bf16[256,3584]{1,0:T(8,128)(2,1)} %g.1) | copy-start | bytes 5505028

commit v2 on v0

v2 whole, which is shorter than its diff:
```python
import math

import jax
import jax.numpy as jnp
from jax import lax
from jax.experimental import pallas as pl
from jax.experimental.pallas import tpu as pltpu
from jax.sharding import PartitionSpec as P

M = 8192
N = 28672
RANK = 256
MU = 90

MESH = pl.DeviceIdType.MESH
HI = lax.Precision.HIGHEST
F32 = jnp.float32
BF16 = jnp.bfloat16
NX, NY, NZ = 4, 4, 8
NF = NX * NY * 2
ROWS = M // NF
COLS = N // NZ
CHUNK = 896
BLOCK = COLS // NF
SENDS = 120
VMEM_LIMIT = 60 * 1024 * 1024


def dot(a, b, ca, cb, precision=None):
    return lax.dot_general(
        a, b, (((ca,), (cb,)), ((), ())), precision=precision, preferred_element_type=F32
    )


def lower_inverse(gram, beside, b=32, s8=8):
    n = gram.shape[0]
    rows = lax.broadcasted_iota(jnp.int32, (8, 128), 0)
    lanes = lax.broadcasted_iota(jnp.int32, (b, n), 1)
    sub = lax.broadcasted_iota(jnp.int32, (b, n), 0)
    panels = [gram[p * b:(p + 1) * b, :] for p in range(n // b)]
    done = []
    tiles = b // 8
    for p in range(n // b):
        r0 = p * b
        P = panels[p]
        nt = n // 128
        home = r0 // 128
        ident = jnp.where(lanes == sub + r0, 1.0, 0.0)[:, home * 128:(home + 1) * 128]
        M = [[P[8 * a:8 * a + 8, 128 * l:128 * l + 128] for l in range(nt)] + [ident[8 * a:8 * a + 8]] for a in range(tiles)]
        piv = [jnp.ones((8, 128), jnp.float32) for _ in range(tiles)]
        for s in range(b // s8):
            a0 = s
            C = []
            for k in range(s8):
                lane = r0 - home * 128 + s * s8 + k
                C.append([jnp.broadcast_to(M[a][home][:, lane:lane + 1], (8, 128)) if a >= a0 else None for a in range(tiles)])
            for j in range(s8):
                sj = jnp.broadcast_to(C[j][a0][j:j + 1, :], (8, 128))
                inv = 1.0 / sj
                w = [None] * tiles
                for a in range(a0, tiles):
                    wa = C[j][a] * inv
                    if a == a0:
                        wa = jnp.where(rows > j, wa, 0.0)
                    w[a] = wa
                for k in range(j + 1, s8):
                    bk = jnp.broadcast_to(C[j][a0][k:k + 1, :], (8, 128))
                    for a in range(a0, tiles):
                        C[k][a] = C[k][a] - w[a] * bk
                piv[a0] = jnp.where(rows == j, sj, piv[a0])
                for l in range(nt + 1):
                    row = jnp.broadcast_to(M[a0][l][j:j + 1, :], (8, 128))
                    for a in range(a0, tiles):
                        M[a][l] = M[a][l] - w[a] * row
        rs = [lax.rsqrt(v) for v in piv]
        full = []
        for a in range(tiles):
            out = [M[a][l] * rs[a] for l in range(nt + 1)]
            z = out.pop()
            ln = lax.broadcasted_iota(jnp.int32, (8, 128), 1) + home * 128
            out[home] = jnp.where((ln >= r0) & (ln < r0 + b), z, out[home])
            full.append(jnp.concatenate(out, axis=1))
        U = jnp.concatenate(full, axis=0)
        done.append(U)
        if p + 1 < n // b:
            r1 = r0 + b
            upd = lax.dot_general(U, U, (((0,), (0,)), ((), ())), precision=HI, preferred_element_type=jnp.float32)
            for q in range(p + 1, n // b):
                old = jnp.where((lanes >= r0) & (lanes < r1), 0.0, panels[q])
                panels[q] = old - upd[q * b:(q + 1) * b, :]
        if p in beside:
            beside[p]()
    W = jnp.concatenate(done, axis=0)
    li = lax.broadcasted_iota(jnp.int32, (n, n), 1)
    si = lax.broadcasted_iota(jnp.int32, (n, n), 0)
    return jnp.where(li <= si, W, 0.0)


def step_kernel(g_hbm, m_hbm, b_hbm, out, squares, ortho, gbuf, mbuf, bbuf, bht, part, rz, left, gpart, gc, gsum, rg, own, r2,
                gram, r, rc, f1, sab, f2, sq, qc, qx, qy, qz, load, ssem, rsem):
    f = lax.axis_index("fsdp")
    t = lax.axis_index("tp")
    core = lax.rem(f, 2)
    x = lax.rem(f // 2, NX)
    y = f // (2 * NX)
    other = 1 - core
    nc = COLS // CHUNK

    def dev(px, py, pc):
        return ((py * NX + px) * 2 + pc, t)

    xs = [lax.rem(x + j, NX) for j in range(NX)]
    ys = [lax.rem(y + j, NY) for j in range(NY)]
    zs = [lax.rem(t + j, NZ) for j in range(NZ)]
    sibling = dev(x, y, other)
    plane = [(i, j) for i in range(NX) for j in range(NY) if (i, j) != (0, 0)]
    loads = []
    for c in range(nc):
        cols = pl.ds(c * CHUNK, CHUNK)
        three = [
            pltpu.make_async_copy(b_hbm.at[cols, :], bbuf.at[cols, :], load.at[3 * c]),
            pltpu.make_async_copy(g_hbm.at[:, cols], gbuf.at[:, cols], load.at[3 * c + 1]),
            pltpu.make_async_copy(m_hbm.at[:, cols], mbuf.at[:, cols], load.at[3 * c + 2]),
        ]
        for cp in three:
            cp.start()
        loads.append(three)
    barrier = pltpu.get_barrier_semaphore()
    for j in range(1, NZ):
        pl.semaphore_signal(barrier, inc=1, device_id=(f, zs[j]), device_id_type=MESH)
    for i, j in plane:
        pl.semaphore_signal(barrier, inc=1, device_id=dev(xs[i], ys[j], core), device_id_type=MESH)
    pl.semaphore_signal(barrier, inc=1, device_id=sibling, device_id_type=MESH)

    sends = []

    def exchange(src, dst, device):
        k = len(sends)
        cp = pltpu.make_async_remote_copy(
            src_ref=src, dst_ref=dst, send_sem=ssem.at[k], recv_sem=rsem.at[k], device_id=device, device_id_type=MESH
        )
        cp.start()
        sends.append(cp)
        return cp

    def share(ref, device):
        return exchange(ref, ref, device)

    def piece(z, size):
        return pl.ds(pl.multiple_of(z * size, size), size)

    for c in range(nc):
        for cp in loads[c]:
            cp.wait()
        cols = pl.ds(c * CHUNK, CHUNK)
        half = (mbuf[:, cols].astype(F32) + gbuf[:, cols].astype(F32)).astype(BF16)
        gbuf[:, cols] = half
        term = dot(half, bbuf[cols, :], 1, 0)
        if c == 0:
            part[...] = term
        else:
            part[...] += term
    part[...] = part[...] * (1.0 / math.sqrt(N))
    pl.semaphore_wait(barrier, NZ + len(plane))

    zr = ROWS // NZ
    cps = [exchange(part.at[piece(zs[j], zr), :], rz.at[j - 1], (f, zs[j])) for j in range(1, NZ)]
    for c in range(nc):
        cols = pl.ds(c * CHUNK, CHUNK)
        bht[cols, :] = gbuf[:, cols].T
    mine = part[piece(t, zr), :]
    for j in range(1, NZ):
        cps[j - 1].wait_recv()
        mine = mine + rz[j - 1]
    left[piece(t, zr), :] = mine

    def z_block(j):
        return left.at[piece(zs[j % NZ], zr), :]

    def z_half(j, k):
        return left.at[pl.ds(pl.multiple_of(zs[j % NZ] * zr + k * (zr // 2), zr // 2), zr // 2), :]

    up, down = (f, zs[1]), (f, zs[NZ - 1])
    az = [(share(z_block(0), up), share(z_block(0), down))]

    def z_step(k):
        az[-1][0].wait_recv()
        az[-1][1].wait_recv()
        if k < 3:
            az.append((share(z_block(NZ - k), up), share(z_block(k), down)))
        else:
            az.append((share(z_half(NZ - k, 0), up), share(z_half(k, 1), down)))

    gh = RANK // 2
    gr = gh // (NX * NY)
    gpart[...] = dot(mine, mine, 0, 0, HI)
    cp = exchange(gpart.at[piece(other, gh), :], gc, sibling)
    cp.wait_recv()
    gsum[...] = gpart[piece(core, gh), :] + gc[...]
    cps = [
        exchange(gsum.at[piece(ys[j] * NX + xs[i], gr), :], rg.at[k], dev(xs[i], ys[j], core))
        for k, (i, j) in enumerate(plane)
    ]
    z_step(1)
    acc = gsum[piece(y * NX + x, gr), :]
    for k, cp in enumerate(cps):
        cp.wait_recv()
        acc = acc + rg[k]
    own[...] = acc
    cps = [exchange(own, r2.at[j - 1], (f, zs[j])) for j in range(1, NZ)]
    z_step(2)
    for j in range(1, NZ):
        cps[j - 1].wait_recv()
        acc = acc + r2[j - 1]
    grow = pl.ds(pl.multiple_of(core * gh + (y * NX + x) * gr, gr), gr)
    gram[grow, :] = acc
    cps = [share(gram.at[grow, :], dev(xs[i], ys[j], core)) for i, j in plane]
    z_step(3)
    az[-1][0].wait_recv()
    az[-1][1].wait_recv()

    hi = left[...].astype(BF16)
    lo = (left[...] - hi.astype(F32)).astype(BF16)
    wide = COLS // 2
    nk = wide // CHUNK
    qk = NX // nk

    def product(k, pc):
        half = bht[pl.ds(pl.multiple_of(pc * wide + k * CHUNK, 128), CHUNK), :]
        val = dot(half, hi, 1, 0) + dot(half, lo, 1, 0)
        for h in range(2):
            r[h, pc, k * qk:(k + 1) * qk] = val[:, 128 * h:128 * h + 128].reshape(qk, NY, BLOCK, 128)

    cc = []
    for k in range(nk):
        product(k, other)
        qs = pl.ds(k * qk, qk)
        cc.append([exchange(r.at[h, other, qs], rc.at[h, qs], sibling) for h in range(2)])
    for cp in cps:
        cp.wait_recv()
    cg = share(gram.at[piece(core, gh), :], sibling)
    for k in range(nk):
        product(k, core)
    cg.wait_recv()

    east, west = dev(xs[1], y, core), dev(xs[3], y, core)
    north, south = dev(x, ys[1], core), dev(x, ys[3], core)
    ways = ((xs, east, west), (ys, north, south))
    state = {}

    def scatter_begin(name, axis, view, land):
        pos, nxt, prv = ways[axis]
        state[name] = [
            exchange(view(pos[2], 0), land(0), nxt),
            exchange(view(pos[2], 1), land(1), prv),
            exchange(view(pos[1], 1), land(2), nxt),
            exchange(view(pos[3], 0), land(3), prv),
        ]

    def scatter_relay(name, axis, view, land):
        pos, nxt, prv = ways[axis]
        cps = state[name]
        for k, (q, to) in enumerate(((pos[1], nxt), (pos[3], prv))):
            cps[k].wait_recv()
            ref = view(q, k)
            ref[...] = ref[...] + land(k)[...]
            cps.append(exchange(ref, land(4 + k), to))

    def scatter_end(name, axis, view, land):
        pos = ways[axis][0]
        cps = state[name]
        for k in range(2, 6):
            cps[k].wait_recv()
        return (
            view(pos[0], 0)[...] + land(3)[...] + land(4)[...],
            view(pos[0], 1)[...] + land(2)[...] + land(5)[...],
        )

    def first(h):
        def view(q, k):
            return r.at[0, core, q, pl.ds(2 * k, 2)] if h == 0 else r.at[1, core, pl.ds(2 * k, 2), q]
        return ("first", h), h, view, lambda k: f1.at[h, k]

    def second(h):
        size = BLOCK // 2
        return ("second", h), 1 - h, lambda q, k: sab.at[h, q, pl.ds(k * size, size)], lambda k: f2.at[h, k]

    def begin_first():
        for k in range(nk):
            qs = pl.ds(k * qk, qk)
            for h in range(2):
                cc[k][h].wait_recv()
                r[h, core, qs] = r[h, core, qs] + rc[h, qs]
        for h in range(2):
            scatter_begin(*first(h))

    def relay_first():
        for h in range(2):
            scatter_relay(*first(h))

    w = lower_inverse(gram[...], {0: begin_first, 4: relay_first})
    for h in range(2):
        lower, upper = scatter_end(*first(h))
        sab[h, 0:2] = lower
        sab[h, 2:4] = upper
        scatter_begin(*second(h))
    for h in range(2):
        scatter_relay(*second(h))
    halves = [jnp.concatenate(scatter_end(*second(h)), axis=0) for h in range(2)]
    right = dot(jnp.concatenate(halves, axis=1), w, 1, 1, HI)
    total = jnp.sum(right * right, axis=0, keepdims=True)
    srow = lax.broadcasted_iota(jnp.int32, (8, 128), 0)
    sq[...] = jnp.where(srow == 0, total[:, :128], total[:, 128:])
    rounded = right.astype(BF16)
    for h in range(2):
        out[h, core, x, y] = rounded[:, 128 * h:128 * h + 128]

    def gather_begin(axis, whole):
        pos, nxt, prv = ways[axis]
        return [share(whole(pos[0]), nxt), share(whole(pos[0]), prv)]

    def gather_relay(axis, cps, part_of):
        pos, nxt, prv = ways[axis]
        cps[0].wait_recv()
        a = share(part_of(pos[3], 0), nxt)
        cps[1].wait_recv()
        b = share(part_of(pos[1], 1), prv)
        return [a, b]

    cut = 64

    def block(h):
        return (lambda q: out.at[0, core, x, q]) if h == 0 else (lambda q: out.at[1, core, q, y])

    def block_part(h):
        rows = (pl.ds(0, cut), pl.ds(cut, BLOCK - cut))
        if h == 0:
            return lambda q, k: out.at[0, core, x, q, rows[k]]
        return lambda q, k: out.at[1, core, q, y, rows[k]]

    def band(h):
        return (lambda q: out.at[0, core, q]) if h == 0 else (lambda q: out.at[1, core, :, q])

    def band_part(h):
        if h == 0:
            return lambda q, k: out.at[0, core, q, pl.ds(2 * k, 2)]
        return lambda q, k: out.at[1, core, pl.ds(2 * k, 2), q]

    sc = exchange(sq, qc, sibling)
    ag = [gather_begin(1 - h, block(h)) for h in range(2)]
    sc.wait_recv()
    qx[x] = sq[...] + qc[...]
    sx = [share(qx.at[x], dev(xs[j], y, core)) for j in range(1, NX)]
    ag = [gather_relay(1 - h, ag[h], block_part(h)) for h in range(2)]
    for cp in sx:
        cp.wait_recv()
    qy[y] = qx[0] + qx[1] + qx[2] + qx[3]
    sy = [share(qy.at[y], dev(x, ys[j], core)) for j in range(1, NY)]
    last = []
    begun = []
    for h in range(2):
        for cp in ag[h]:
            cp.wait_recv()
        begun.append(gather_begin(h, band(h)))
        last.append(share(band(h)(ways[h][0][0]), sibling))
    for cp in sy:
        cp.wait_recv()
    qz[t] = qy[0] + qy[1] + qy[2] + qy[3]
    sz = [share(qz.at[t], (f, zs[j])) for j in range(1, NZ)]
    ortho[...] = dot(left[...], w, 1, 1, HI).astype(BF16)
    ag = [gather_relay(h, begun[h], band_part(h)) for h in range(2)]
    for h in range(2):
        for k in (3, 1):
            last.append(share(band(h)(ways[h][0][k]), sibling))
    for cp in sz:
        cp.wait_recv()
    total = qz[0]
    for j in range(1, NZ):
        total = total + qz[j]
    squares[...] = total
    for h in range(2):
        for cp in ag[h]:
            cp.wait_recv()
        last.append(share(band(h)(ways[h][0][2]), sibling))
    for cp in last:
        cp.wait_recv()
    for cp in sends:
        cp.wait_send()


def output_kernel(g, m, ortho, right, squares, update, new_momentum, new_basis):
    total = jnp.concatenate([squares[0:1, :], squares[1:2, :]], axis=1)
    scale = jnp.sqrt(total / N + 1e-06)
    rr = jnp.concatenate([right[0], right[1]], axis=1).astype(F32)
    nb = (rr / scale).astype(BF16)
    new_basis[...] = nb
    scaled = (ortho[...].astype(F32) * scale).astype(BF16)
    lowrank = dot(scaled, nb, 1, 1)
    buffer = m[...].astype(F32) + g[...].astype(F32)
    new_momentum[...] = (buffer - (1.0 - MU / 100.0) * lowrank).astype(BF16)
    update[...] = (dot(ortho[...], nb, 1, 1) * math.sqrt(M / RANK)).astype(BF16)


def body(grad, momentum, basis):
    anywhere = pl.BlockSpec(memory_space=pl.ANY)
    vmem = pl.BlockSpec(memory_space=pltpu.VMEM)
    dma = pltpu.SemaphoreType.DMA
    zr = ROWS // NZ
    gh = RANK // 2
    gr = gh // (NX * NY)
    right, squares, ortho = pl.pallas_call(
        step_kernel,
        out_shape=(
            jax.ShapeDtypeStruct((2, 2, NX, NY, BLOCK, 128), BF16),
            jax.ShapeDtypeStruct((8, 128), F32),
            jax.ShapeDtypeStruct((ROWS, RANK), BF16),
        ),
        in_specs=[anywhere] * 3,
        out_specs=(vmem, vmem, vmem),
        scratch_shapes=[
            pltpu.VMEM((ROWS, COLS), BF16), pltpu.VMEM((ROWS, COLS), BF16), pltpu.VMEM((COLS, RANK), BF16),
            pltpu.VMEM((COLS, RANK), BF16),
            pltpu.VMEM((ROWS, RANK), F32), pltpu.VMEM((NZ - 1, zr, RANK), F32), pltpu.VMEM((ROWS, RANK), F32),
            pltpu.VMEM((RANK, RANK), F32), pltpu.VMEM((gh, RANK), F32), pltpu.VMEM((gh, RANK), F32),
            pltpu.VMEM((NX * NY - 1, gr, RANK), F32), pltpu.VMEM((gr, RANK), F32), pltpu.VMEM((NZ - 1, gr, RANK), F32),
            pltpu.VMEM((RANK, RANK), F32),
            pltpu.VMEM((2, 2, NX, NY, BLOCK, 128), F32), pltpu.VMEM((2, NX, NY, BLOCK, 128), F32),
            pltpu.VMEM((2, 6, 2, BLOCK, 128), F32), pltpu.VMEM((2, NX, BLOCK, 128), F32),
            pltpu.VMEM((2, 6, BLOCK // 2, 128), F32),
            pltpu.VMEM((8, 128), F32), pltpu.VMEM((8, 128), F32),
            pltpu.VMEM((NX, 8, 128), F32), pltpu.VMEM((NY, 8, 128), F32), pltpu.VMEM((NZ, 8, 128), F32),
            dma((3 * (COLS // CHUNK),)), dma((SENDS,)), dma((SENDS,)),
        ],
        compiler_params=pltpu.CompilerParams(collective_id=0, has_side_effects=True, vmem_limit_bytes=VMEM_LIMIT),
        name="step_kernel",
    )(grad, momentum, basis)
    step = 512
    return pl.pallas_call(
        output_kernel,
        grid=(COLS // step,),
        out_shape=(
            jax.ShapeDtypeStruct((ROWS, COLS), BF16),
            jax.ShapeDtypeStruct((ROWS, COLS), BF16),
            jax.ShapeDtypeStruct((COLS, RANK), BF16),
        ),
        in_specs=[
            pl.BlockSpec((ROWS, step), lambda i: (0, i)),
            pl.BlockSpec((ROWS, step), lambda i: (0, i)),
            pl.BlockSpec((ROWS, RANK), lambda i: (0, 0)),
            pl.BlockSpec((2, step, 128), lambda i: (0, i, 0)),
            pl.BlockSpec((8, 128), lambda i: (0, 0)),
        ],
        out_specs=(
            pl.BlockSpec((ROWS, step), lambda i: (0, i)),
            pl.BlockSpec((ROWS, step), lambda i: (0, i)),
            pl.BlockSpec((step, RANK), lambda i: (i, 0)),
        ),
        compiler_params=pltpu.CompilerParams(vmem_limit_bytes=VMEM_LIMIT),
        name="output_kernel",
    )(grad, momentum, ortho, right.reshape(2, COLS, 128), squares)


def solution(mesh):
    placed = (P("fsdp", "tp"), P("fsdp", "tp"), P("tp", None))
    return jax.shard_map(
        body,
        mesh=mesh,
        in_specs=placed,
        out_specs=(P("fsdp", "tp"), P("fsdp", "tp"), P("tp", None)),
        check_vma=False,
    )
```

time: 425 us -> 94.3 us (0.22)
  waiting for transfers between devices: 309 us -> 0 us
  Pallas kernels: 0 us -> 93.1 us
  other arithmetic: 59.7 us -> 0 us
  matrix products: 16 us -> 0 us
  between operations: 15.2 us -> 0.64 us
  blocking collectives: 13.7 us -> 0 us
  local copies, waits for them, and re-layouts: 7.23 us -> 0 us
    psum x3 -> x0, waiting for transfers between devices: 308 us -> none  [the longest x1 121 us: body(): right = lax.psum(partial_right, 'fsdp')]
    pallas_call x0 -> x2, Pallas kernels: none -> 93.1 us  [the longest x1 84.8 us: body(): pl.pallas_call(step_kernel, out_shape=(jax.ShapeDtypeStruct((2, 2, NX, NY...]
    another operation x9 -> x0, other arithmetic: 53.7 us -> none  [the longest x6 34 us: orthonormal(): lower = jnp.linalg.cholesky(gram)]
    dot_general x5 -> x0, matrix products: 14.5 us -> none  [the longest x1 4.58 us: body(): lax.dot_general(buffer_half, ortho, (((0,), (0,)), ((), ())), preferred_e...]
    psum x1 -> x0, blocking collectives: 13.7 us -> none  [body(): squares = lax.psum(jnp.sum(right * right, axis=0), 'tp')]
  transfers between devices with their start and end apart: 3 -> 0, of which waited for: 3 -> 0; matrix products, arithmetic and copies ran while one was open for 0% -> 0% of each run, Pallas kernels for 0% -> 0%
where the time goes in v2:
time: 94.3 us; the launch traced here: 93.7 us
  Pallas kernels  93.1 us (99%)
    pallas_call x1, Pallas kernels, body(): pl.pallas_call(step_kernel, out_shape=(jax.ShapeDtypeStruct((2, 2, NX, NY...  84.8 us
    pallas_call x1, Pallas kernels, body(): pl.pallas_call(output_kernel, grid=(COLS // step,), out_shape=(jax.ShapeD...  8.31 us

profile of v2, /device:TPU:1, one launch (start us, length us, event | category | flops | bytes accessed | tf_op | source)
XLA Modules:
  0.0 93.7 jit_solution(12385985517180406199)
XLA Ops:
  0.6 84.8 %step_kernel.1 = (bf16[2,2,4,4,112,128]{5,4,3,2,1,0:T(8,128)(2,1)}, f32[8,128]{1,0:T(8,128)}, bf16[256,256]{1,0:T(8,128)(2,1)}) custom-call(bf16[256,3584]{1,0:T(8,128)(2,1)} %g.1, bf16[256,3584]{1,0:T(8,128)(2,1)} %m.1, bf16[3584,256]{1,0:T(8,128)(2,1)} %b_hbm.1), custom_call_target="tpu_custom_call" | custom-call | tf_op jit(solution)/shard_map/step_kernel/pallas_call | solution.py:411
  85.4 8.3 %output_kernel.1 = (bf16[256,3584]{1,0:T(8,128)(2,1)}, bf16[256,3584]{1,0:T(8,128)(2,1)}, bf16[3584,256]{1,0:T(8,128)(2,1)}) custom-call(bf16[256,3584]{1,0:T(8,128)(2,1)} %g.1, bf16[256,3584]{1,0:T(8,128)(2,1)} %m.1, bf16[256,256]{1,0:T(8,128)(2,1)} %get-tuple-element.6.ortho, bf16[2,3584,128]{2,1,0:T(8,128)(2,1)} %bitcast.1, f32[8,128]{1,0:T(8,128)} %get-tuple-element.8.squares), custom_call_target="tpu_custom_call" | custom-call | tf_op jit(solution)/shard_map/output_kernel/pallas_call | solution.py:438

commit v3 on v2

--- a/solution.py
+++ b/solution.py
@@ -22,7 +22,6 @@
 COLS = N // NZ
 CHUNK = 896
 BLOCK = COLS // NF
-SENDS = 120
 VMEM_LIMIT = 60 * 1024 * 1024
 
 
@@ -96,24 +95,65 @@
     return jnp.where(li <= si, W, 0.0)
 
 
-def step_kernel(g_hbm, m_hbm, b_hbm, out, squares, ortho, gbuf, mbuf, bbuf, bht, part, rz, left, gpart, gc, gsum, rg, own, r2,
-                gram, r, rc, f1, sab, f2, sq, qc, qx, qy, qz, load, ssem, rsem):
-    f = lax.axis_index("fsdp")
-    t = lax.axis_index("tp")
-    core = lax.rem(f, 2)
-    x = lax.rem(f // 2, NX)
-    y = f // (2 * NX)
-    other = 1 - core
+class Place:
+    def __init__(self, ssem, rsem):
+        self.ssem, self.rsem = ssem, rsem
+        self.sends = []
+        self.f = lax.axis_index("fsdp")
+        self.t = lax.axis_index("tp")
+        self.core = lax.rem(self.f, 2)
+        self.other = 1 - self.core
+        self.x = lax.rem(self.f // 2, NX)
+        self.y = self.f // (2 * NX)
+        self.xs = [lax.rem(self.x + j, NX) for j in range(NX)]
+        self.ys = [lax.rem(self.y + j, NY) for j in range(NY)]
+        self.zs = [lax.rem(self.t + j, NZ) for j in range(NZ)]
+        self.sibling = self.dev(self.x, self.y, self.other)
+        self.zdev = [(self.f, z) for z in self.zs]
+        self.plane = [
+            self.dev(self.xs[i], self.ys[j], self.core) for i in range(NX) for j in range(NY) if (i, j) != (0, 0)
+        ]
+        self.chips = [self.ys[j] * NX + self.xs[i] for i in range(NX) for j in range(NY) if (i, j) != (0, 0)]
+        self.chip = self.y * NX + self.x
+        self.ways = (
+            (self.xs, self.dev(self.xs[1], self.y, self.core), self.dev(self.xs[3], self.y, self.core)),
+            (self.ys, self.dev(self.x, self.ys[1], self.core), self.dev(self.x, self.ys[3], self.core)),
+        )
+
+    def dev(self, px, py, pc):
+        return ((py * NX + px) * 2 + pc, self.t)
+
+    def greet(self, devices):
+        barrier = pltpu.get_barrier_semaphore()
+        for device in devices:
+            pl.semaphore_signal(barrier, inc=1, device_id=device, device_id_type=MESH)
+        return lambda: pl.semaphore_wait(barrier, len(devices))
+
+    def exchange(self, src, dst, device):
+        k = len(self.sends)
+        cp = pltpu.make_async_remote_copy(
+            src_ref=src, dst_ref=dst, send_sem=self.ssem.at[k], recv_sem=self.rsem.at[k],
+            device_id=device, device_id_type=MESH,
+        )
+        cp.start()
+        self.sends.append(cp)
+        return cp
+
+    def share(self, ref, device):
+        return self.exchange(ref, ref, device)
+
+    def finish(self):
+        for cp in self.sends:
+            cp.wait_send()
+
+
+def piece(z, size):
+    return pl.ds(pl.multiple_of(z * size, size), size)
+
+
+def left_kernel(g_hbm, m_hbm, b_hbm, left, bht, gbuf, mbuf, bbuf, part, rz, load, ssem, rsem):
+    at = Place(ssem, rsem)
     nc = COLS // CHUNK
-
-    def dev(px, py, pc):
-        return ((py * NX + px) * 2 + pc, t)
-
-    xs = [lax.rem(x + j, NX) for j in range(NX)]
-    ys = [lax.rem(y + j, NY) for j in range(NY)]
-    zs = [lax.rem(t + j, NZ) for j in range(NZ)]
-    sibling = dev(x, y, other)
-    plane = [(i, j) for i in range(NX) for j in range(NY) if (i, j) != (0, 0)]
     loads = []
     for c in range(nc):
         cols = pl.ds(c * CHUNK, CHUNK)
@@ -125,30 +165,8 @@
         for cp in three:
             cp.start()
         loads.append(three)
-    barrier = pltpu.get_barrier_semaphore()
-    for j in range(1, NZ):
-        pl.semaphore_signal(barrier, inc=1, device_id=(f, zs[j]), device_id_type=MESH)
-    for i, j in plane:
-        pl.semaphore_signal(barrier, inc=1, device_id=dev(xs[i], ys[j], core), device_id_type=MESH)
-    pl.semaphore_signal(barrier, inc=1, device_id=sibling, device_id_type=MESH)
-
-    sends = []
-
-    def exchange(src, dst, device):
-        k = len(sends)
-        cp = pltpu.make_async_remote_copy(
-            src_ref=src, dst_ref=dst, send_sem=ssem.at[k], recv_sem=rsem.at[k], device_id=device, device_id_type=MESH
-        )
-        cp.start()
-        sends.append(cp)
-        return cp
-
-    def share(ref, device):
-        return exchange(ref, ref, device)
-
-    def piece(z, size):
-        return pl.ds(pl.multiple_of(z * size, size), size)
-
+    ready = at.greet(at.zdev[1:])
+    total = None
     for c in range(nc):
         for cp in loads[c]:
             cp.wait()
@@ -156,69 +174,73 @@
         half = (mbuf[:, cols].astype(F32) + gbuf[:, cols].astype(F32)).astype(BF16)
         gbuf[:, cols] = half
         term = dot(half, bbuf[cols, :], 1, 0)
-        if c == 0:
-            part[...] = term
-        else:
-            part[...] += term
-    part[...] = part[...] * (1.0 / math.sqrt(N))
-    pl.semaphore_wait(barrier, NZ + len(plane))
-
+        total = term if c == 0 else total + term
+    part[...] = (total * (1.0 / math.sqrt(N))).astype(BF16)
+    ready()
     zr = ROWS // NZ
-    cps = [exchange(part.at[piece(zs[j], zr), :], rz.at[j - 1], (f, zs[j])) for j in range(1, NZ)]
+    cps = [at.exchange(part.at[piece(at.zs[j], zr), :], rz.at[j - 1], at.zdev[j]) for j in range(1, NZ)]
     for c in range(nc):
         cols = pl.ds(c * CHUNK, CHUNK)
         bht[cols, :] = gbuf[:, cols].T
-    mine = part[piece(t, zr), :]
+    mine = part[piece(at.t, zr), :].astype(F32)
     for j in range(1, NZ):
         cps[j - 1].wait_recv()
-        mine = mine + rz[j - 1]
-    left[piece(t, zr), :] = mine
+        mine = mine + rz[j - 1].astype(F32)
+    left[piece(at.t, zr), :] = mine
 
     def z_block(j):
-        return left.at[piece(zs[j % NZ], zr), :]
+        return left.at[piece(at.zs[j % NZ], zr), :]
 
     def z_half(j, k):
-        return left.at[pl.ds(pl.multiple_of(zs[j % NZ] * zr + k * (zr // 2), zr // 2), zr // 2), :]
-
-    up, down = (f, zs[1]), (f, zs[NZ - 1])
-    az = [(share(z_block(0), up), share(z_block(0), down))]
-
-    def z_step(k):
-        az[-1][0].wait_recv()
-        az[-1][1].wait_recv()
+        return left.at[pl.ds(pl.multiple_of(at.zs[j % NZ] * zr + k * (zr // 2), zr // 2), zr // 2), :]
+
+    up, down = at.zdev[1], at.zdev[NZ - 1]
+    now = (at.share(z_block(0), up), at.share(z_block(0), down))
+    for k in range(1, 4):
+        now[0].wait_recv()
+        now[1].wait_recv()
         if k < 3:
-            az.append((share(z_block(NZ - k), up), share(z_block(k), down)))
+            now = (at.share(z_block(NZ - k), up), at.share(z_block(k), down))
         else:
-            az.append((share(z_half(NZ - k, 0), up), share(z_half(k, 1), down)))
-
+            now = (at.share(z_half(NZ - k, 0), up), at.share(z_half(k, 1), down))
+    now[0].wait_recv()
+    now[1].wait_recv()
+    at.finish()
+
+
+def gram_kernel(left, gram, gpart, gc, gsum, rg, own, r2, ssem, rsem):
+    at = Place(ssem, rsem)
+    ready = at.greet(at.zdev[1:] + at.plane + [at.sibling])
+    zr = ROWS // NZ
     gh = RANK // 2
     gr = gh // (NX * NY)
+    mine = left[piece(at.t, zr), :]
     gpart[...] = dot(mine, mine, 0, 0, HI)
-    cp = exchange(gpart.at[piece(other, gh), :], gc, sibling)
-    cp.wait_recv()
-    gsum[...] = gpart[piece(core, gh), :] + gc[...]
-    cps = [
-        exchange(gsum.at[piece(ys[j] * NX + xs[i], gr), :], rg.at[k], dev(xs[i], ys[j], core))
-        for k, (i, j) in enumerate(plane)
-    ]
-    z_step(1)
-    acc = gsum[piece(y * NX + x, gr), :]
+    ready()
+    at.exchange(gpart.at[piece(at.other, gh), :], gc, at.sibling).wait_recv()
+    gsum[...] = gpart[piece(at.core, gh), :] + gc[...]
+    cps = [at.exchange(gsum.at[piece(at.chips[k], gr), :], rg.at[k], device) for k, device in enumerate(at.plane)]
+    acc = gsum[piece(at.chip, gr), :]
     for k, cp in enumerate(cps):
         cp.wait_recv()
         acc = acc + rg[k]
     own[...] = acc
-    cps = [exchange(own, r2.at[j - 1], (f, zs[j])) for j in range(1, NZ)]
-    z_step(2)
+    cps = [at.exchange(own, r2.at[j - 1], at.zdev[j]) for j in range(1, NZ)]
     for j in range(1, NZ):
         cps[j - 1].wait_recv()
         acc = acc + r2[j - 1]
-    grow = pl.ds(pl.multiple_of(core * gh + (y * NX + x) * gr, gr), gr)
+    grow = pl.ds(pl.multiple_of(at.core * gh + at.chip * gr, gr), gr)
     gram[grow, :] = acc
-    cps = [share(gram.at[grow, :], dev(xs[i], ys[j], core)) for i, j in plane]
-    z_step(3)
-    az[-1][0].wait_recv()
-    az[-1][1].wait_recv()
-
+    cps = [at.share(gram.at[grow, :], device) for device in at.plane]
+    for cp in cps:
+        cp.wait_recv()
+    at.share(gram.at[piece(at.core, gh), :], at.sibling).wait_recv()
+    at.finish()
+
+
+def scatter_kernel(gram, left, bht, shard, ortho, r, rc, f1, sab, f2, ssem, rsem):
+    at = Place(ssem, rsem)
+    ready = at.greet([at.sibling, *at.ways[0][1:], *at.ways[1][1:]])
     hi = left[...].astype(BF16)
     lo = (left[...] - hi.astype(F32)).astype(BF16)
     wide = COLS // 2
@@ -232,20 +254,17 @@
             r[h, pc, k * qk:(k + 1) * qk] = val[:, 128 * h:128 * h + 128].reshape(qk, NY, BLOCK, 128)
 
     cc = []
+    core, other, sibling, exchange = at.core, at.other, at.sibling, at.exchange
     for k in range(nk):
         product(k, other)
+        if k == 0:
+            ready()
         qs = pl.ds(k * qk, qk)
         cc.append([exchange(r.at[h, other, qs], rc.at[h, qs], sibling) for h in range(2)])
-    for cp in cps:
-        cp.wait_recv()
-    cg = share(gram.at[piece(core, gh), :], sibling)
     for k in range(nk):
         product(k, core)
-    cg.wait_recv()
-
-    east, west = dev(xs[1], y, core), dev(xs[3], y, core)
-    north, south = dev(x, ys[1], core), dev(x, ys[3], core)
-    ways = ((xs, east, west), (ys, north, south))
+
+    ways = at.ways
     state = {}
 
     def scatter_begin(name, axis, view, land):
@@ -308,12 +327,27 @@
         scatter_relay(*second(h))
     halves = [jnp.concatenate(scatter_end(*second(h)), axis=0) for h in range(2)]
     right = dot(jnp.concatenate(halves, axis=1), w, 1, 1, HI)
+    shard[...] = right
+    ortho[...] = dot(left[...], w, 1, 1, HI).astype(BF16)
+    at.finish()
+
+
+def gather_kernel(shard, out, squares, sq, qc, qx, qy, qz, ssem, rsem):
+    at = Place(ssem, rsem)
+    ready = at.greet(
+        at.zdev[1:] + [at.sibling]
+        + [at.dev(at.xs[j], at.y, at.core) for j in range(1, NX)] + [at.dev(at.x, at.ys[j], at.core) for j in range(1, NY)]
+    )
+    core, sibling, exchange, share, dev, ways = at.core, at.sibling, at.exchange, at.share, at.dev, at.ways
+    x, y, t, f, xs, ys, zs = at.x, at.y, at.t, at.f, at.xs, at.ys, at.zs
+    right = shard[...]
     total = jnp.sum(right * right, axis=0, keepdims=True)
     srow = lax.broadcasted_iota(jnp.int32, (8, 128), 0)
     sq[...] = jnp.where(srow == 0, total[:, :128], total[:, 128:])
     rounded = right.astype(BF16)
     for h in range(2):
         out[h, core, x, y] = rounded[:, 128 * h:128 * h + 128]
+    ready()
 
     def gather_begin(axis, whole):
         pos, nxt, prv = ways[axis]
@@ -367,7 +401,6 @@
         cp.wait_recv()
     qz[t] = qy[0] + qy[1] + qy[2] + qy[3]
     sz = [share(qz.at[t], (f, zs[j])) for j in range(1, NZ)]
-    ortho[...] = dot(left[...], w, 1, 1, HI).astype(BF16)
     ag = [gather_relay(h, begun[h], band_part(h)) for h in range(2)]
     for h in range(2):
         for k in (3, 1):
@@ -384,8 +417,7 @@
         last.append(share(band(h)(ways[h][0][2]), sibling))
     for cp in last:
         cp.wait_recv()
-    for cp in sends:
-        cp.wait_send()
+    at.finish()
 
 
 def output_kernel(g, m, ortho, right, squares, update, new_momentum, new_basis):
@@ -395,46 +427,56 @@
     nb = (rr / scale).astype(BF16)
     new_basis[...] = nb
     scaled = (ortho[...].astype(F32) * scale).astype(BF16)
-    lowrank = dot(scaled, nb, 1, 1)
+    both = dot(jnp.concatenate([scaled, ortho[...]], axis=0), nb.T, 1, 0)
+    lowrank = both[:ROWS]
     buffer = m[...].astype(F32) + g[...].astype(F32)
     new_momentum[...] = (buffer - (1.0 - MU / 100.0) * lowrank).astype(BF16)
-    update[...] = (dot(ortho[...], nb, 1, 1) * math.sqrt(M / RANK)).astype(BF16)
+    update[...] = (both[ROWS:] * math.sqrt(M / RANK)).astype(BF16)
+
+
+def call(kernel, ident, outs, ins, scratch, sends, loads=0):
+    dma = pltpu.SemaphoreType.DMA
+    sems = ([dma((loads,))] if loads else []) + [dma((sends,)), dma((sends,))]
+    return pl.pallas_call(
+        kernel,
+        out_shape=tuple(jax.ShapeDtypeStruct(*o) for o in outs),
+        in_specs=[pl.BlockSpec(memory_space=pl.ANY if loads else pltpu.VMEM)] * ins,
+        out_specs=tuple(pl.BlockSpec(memory_space=pltpu.VMEM) for _ in outs),
+        scratch_shapes=[pltpu.VMEM(*v) for v in scratch] + sems,
+        compiler_params=pltpu.CompilerParams(collective_id=ident, has_side_effects=True, vmem_limit_bytes=VMEM_LIMIT),
+        name=kernel.__name__,
+    )
 
 
 def body(grad, momentum, basis):
-    anywhere = pl.BlockSpec(memory_space=pl.ANY)
-    vmem = pl.BlockSpec(memory_space=pltpu.VMEM)
-    dma = pltpu.SemaphoreType.DMA
     zr = ROWS // NZ
     gh = RANK // 2
     gr = gh // (NX * NY)
-    right, squares, ortho = pl.pallas_call(
-        step_kernel,
-        out_shape=(
-            jax.ShapeDtypeStruct((2, 2, NX, NY, BLOCK, 128), BF16),
-            jax.ShapeDtypeStruct((8, 128), F32),
-            jax.ShapeDtypeStruct((ROWS, RANK), BF16),
-        ),
-        in_specs=[anywhere] * 3,
-        out_specs=(vmem, vmem, vmem),
-        scratch_shapes=[
-            pltpu.VMEM((ROWS, COLS), BF16), pltpu.VMEM((ROWS, COLS), BF16), pltpu.VMEM((COLS, RANK), BF16),
-            pltpu.VMEM((COLS, RANK), BF16),
-            pltpu.VMEM((ROWS, RANK), F32), pltpu.VMEM((NZ - 1, zr, RANK), F32), pltpu.VMEM((ROWS, RANK), F32),
-            pltpu.VMEM((RANK, RANK), F32), pltpu.VMEM((gh, RANK), F32), pltpu.VMEM((gh, RANK), F32),
-            pltpu.VMEM((NX * NY - 1, gr, RANK), F32), pltpu.VMEM((gr, RANK), F32), pltpu.VMEM((NZ - 1, gr, RANK), F32),
-            pltpu.VMEM((RANK, RANK), F32),
-            pltpu.VMEM((2, 2, NX, NY, BLOCK, 128), F32), pltpu.VMEM((2, NX, NY, BLOCK, 128), F32),
-            pltpu.VMEM((2, 6, 2, BLOCK, 128), F32), pltpu.VMEM((2, NX, BLOCK, 128), F32),
-            pltpu.VMEM((2, 6, BLOCK // 2, 128), F32),
-            pltpu.VMEM((8, 128), F32), pltpu.VMEM((8, 128), F32),
-            pltpu.VMEM((NX, 8, 128), F32), pltpu.VMEM((NY, 8, 128), F32), pltpu.VMEM((NZ, 8, 128), F32),
-            dma((3 * (COLS // CHUNK),)), dma((SENDS,)), dma((SENDS,)),
+    square = ((RANK, RANK), F32)
+    left, bht = call(
+        left_kernel, 0, [((ROWS, RANK), F32), ((COLS, RANK), BF16)], 3,
+        [((ROWS, COLS), BF16), ((ROWS, COLS), BF16), ((COLS, RANK), BF16), ((ROWS, RANK), BF16), ((NZ - 1, zr, RANK), BF16)],
+        NZ - 1 + 8, 3 * (COLS // CHUNK),
+    )(grad, momentum, basis)
+    (gram,) = call(
+        gram_kernel, 1, [square], 1,
+        [square, ((gh, RANK), F32), ((gh, RANK), F32), ((NX * NY - 1, gr, RANK), F32), ((gr, RANK), F32), ((NZ - 1, gr, RANK), F32)],
+        2 * (NX * NY - 1) + NZ - 1 + 2,
+    )(left)
+    shard, ortho = call(
+        scatter_kernel, 2, [((BLOCK, RANK), F32), ((ROWS, RANK), BF16)], 3,
+        [
+            ((2, 2, NX, NY, BLOCK, 128), F32), ((2, NX, NY, BLOCK, 128), F32),
+            ((2, 6, 2, BLOCK, 128), F32), ((2, NX, BLOCK, 128), F32), ((2, 6, BLOCK // 2, 128), F32),
         ],
-        compiler_params=pltpu.CompilerParams(collective_id=0, has_side_effects=True, vmem_limit_bytes=VMEM_LIMIT),
-        name="step_kernel",
-    )(grad, momentum, basis)
-    step = 512
+        28,
+    )(gram, left, bht)
+    right, squares = call(
+        gather_kernel, 3, [((2, 2, NX, NY, BLOCK, 128), BF16), ((8, 128), F32)], 1,
+        [((8, 128), F32), ((8, 128), F32), ((NX, 8, 128), F32), ((NY, 8, 128), F32), ((NZ, 8, 128), F32)],
+        38,
+    )(shard)
+    step = 896
     return pl.pallas_call(
         output_kernel,
         grid=(COLS // step,),

time: 94.3 us -> 119 us (1.26)
  Pallas kernels: 93.1 us -> 118 us
    pallas_call x1 -> x4, Pallas kernels: 84.8 us -> 112 us  [the longest x1 30.2 us: body(): call(gram_kernel, 1, [square], 1, [square, ((gh, RANK), F32), ((gh, RANK)...]
    pallas_call x1, Pallas kernels: 8.31 us -> 6.14 us  [body(): pl.pallas_call(output_kernel, grid=(COLS // step,), out_shape=(jax.ShapeD...]
where the time goes in v3:
time: 119 us
  Pallas kernels  118 us (99%)
    pallas_call x1, Pallas kernels, body(): call(gram_kernel, 1, [square], 1, [square, ((gh, RANK), F32), ((gh, RANK)...  30.2 us
    pallas_call x1, Pallas kernels, body(): call(scatter_kernel, 2, [((BLOCK, RANK), F32), ((ROWS, RANK), BF16)], 3,...  29.5 us
    pallas_call x1, Pallas kernels, body(): call(gather_kernel, 3, [((2, 2, NX, NY, BLOCK, 128), BF16), ((8, 128), F3...  27 us
    pallas_call x1, Pallas kernels, body(): call(left_kernel, 0, [((ROWS, RANK), F32), ((COLS, RANK), BF16)], 3, [((R...  25.1 us
    pallas_call x1, Pallas kernels, body(): pl.pallas_call(output_kernel, grid=(COLS // step,), out_shape=(jax.ShapeD...  6.14 us

profile of v3, /device:TPU:1, one launch (start us, length us, event | category | flops | bytes accessed | tf_op | source)
XLA Modules:
  0.0 118.7 jit_solution(11625335374822373545)
XLA Ops:
  0.6 25.1 %left_kernel.1 = (f32[256,256]{1,0:T(8,128)}, bf16[3584,256]{1,0:T(8,128)(2,1)}) custom-call(bf16[256,3584]{1,0:T(8,128)(2,1)} %g.1, bf16[256,3584]{1,0:T(8,128)(2,1)} %m.1, bf16[3584,256]{1,0:T(8,128)(2,1)} %b_hbm.1), custom_call_target="tpu_custom_call" | custom-call | tf_op jit(solution)/shard_map/left_kernel/pallas_call | solution.py:456
  25.7 30.2 %gram_kernel.1.gram = f32[256,256]{1,0:T(8,128)} custom-call(f32[256,256]{1,0:T(8,128)} %get-tuple-element.9.left), custom_call_target="tpu_custom_call" | custom-call | tf_op jit(solution)/shard_map/gram_kernel/pallas_call | solution.py:461
  56.0 29.5 %scatter_kernel.1 = (f32[112,256]{1,0:T(8,128)}, bf16[256,256]{1,0:T(8,128)(2,1)}) custom-call(f32[256,256]{1,0:T(8,128)} %gram_kernel.1.gram, f32[256,256]{1,0:T(8,128)} %get-tuple-element.9.left, bf16[3584,256]{1,0:T(8,128)(2,1)} %get-tuple-element.10.bht), custom_call_target="tpu_custom_call" | custom-call | tf_op jit(solution)/shard_map/scatter_kernel/pallas_call | solution.py:466
  85.5 27.0 %gather_kernel.1 = (bf16[2,2,4,4,112,128]{5,4,3,2,1,0:T(8,128)(2,1)}, f32[8,128]{1,0:T(8,128)}) custom-call(f32[112,256]{1,0:T(8,128)} %get-tuple-element.12.shard), custom_call_target="tpu_custom_call" | custom-call | tf_op jit(solution)/shard_map/gather_kernel/pallas_call | solution.py:474
  112.5 6.1 %output_kernel.1 = (bf16[256,3584]{1,0:T(8,128)(2,1)}, bf16[256,3584]{1,0:T(8,128)(2,1)}, bf16[3584,256]{1,0:T(8,128)(2,1)}) custom-call(bf16[256,3584]{1,0:T(8,128)(2,1)} %g.1, bf16[256,3584]{1,0:T(8,128)(2,1)} %m.1, bf16[256,256]{1,0:T(8,128)(2,1)} %get-tuple-element.11.ortho, bf16[2,3584,128]{2,1,0:T(8,128)(2,1)} %bitcast.1, ...), custom_call_target="tpu_custom_call" | custom-call | tf_op jit(solution)/shard_map/output_kernel/pallas_call | solution.py:480

commit v4 on v0

v4 whole, which is shorter than its diff:
```python
import math

import jax
import jax.numpy as jnp
from jax import lax
from jax.experimental import pallas as pl
from jax.experimental.pallas import tpu as pltpu
from jax.sharding import PartitionSpec as P

M = 8192
N = 28672
RANK = 256
MU = 90

MESH = pl.DeviceIdType.MESH
HI = lax.Precision.HIGHEST
F32 = jnp.float32
BF16 = jnp.bfloat16
NX, NY, NZ = 4, 4, 8
NF = NX * NY * 2
ROWS = M // NF
COLS = N // NZ
CHUNK = 896
BLOCK = COLS // NF
VMEM_LIMIT = 60 * 1024 * 1024


def dot(a, b, ca, cb, precision=None):
    return lax.dot_general(
        a, b, (((ca,), (cb,)), ((), ())), precision=precision, preferred_element_type=F32
    )


def lower_inverse(gram, b=64, s8=8):
    n = gram.shape[0]
    tiles = b // 8
    nt = n // 128
    rows = lax.broadcasted_iota(jnp.int32, (8, 128), 0)
    ln = lax.broadcasted_iota(jnp.int32, (8, 128), 1)
    lanes = lax.broadcasted_iota(jnp.int32, (b, n), 1)
    panels = [gram[p * b:(p + 1) * b, :] for p in range(n // b)]
    done = []
    for p in range(n // b):
        r0 = p * b
        home = r0 // 128
        P_ = panels[p]
        M_ = [[P_[8 * a:8 * a + 8, 128 * l:128 * l + 128] for l in range(nt)] for a in range(tiles)]
        for a in range(tiles):
            M_[a].append(jnp.where(ln + home * 128 == rows + (r0 + 8 * a), 1.0, 0.0))
        piv = [jnp.ones((8, 128), F32) for _ in range(tiles)]
        for s in range(b // s8):
            C = []
            for k in range(s8):
                lane = r0 - home * 128 + s * s8 + k
                C.append([
                    jnp.broadcast_to(M_[a][home][:, lane:lane + 1], (8, 128)) if a >= s else None for a in range(tiles)
                ])
            for j in range(s8):
                sj = jnp.broadcast_to(C[j][s][j:j + 1, :], (8, 128))
                near = pl.reciprocal(sj, approx=True)
                inv = near * (2.0 - sj * near)
                w = [C[j][a] * inv if a >= s else None for a in range(tiles)]
                for k in range(j + 1, s8):
                    bk = jnp.broadcast_to(C[j][s][k:k + 1, :], (8, 128))
                    for a in range(s, tiles):
                        C[k][a] = C[k][a] - w[a] * bk
                w[s] = jnp.where(rows > j, w[s], 0.0)
                piv[s] = jnp.where(rows == j, sj, piv[s])
                for l in range(nt + 1):
                    row = jnp.broadcast_to(M_[s][l][j:j + 1, :], (8, 128))
                    for a in range(s, tiles):
                        M_[a][l] = M_[a][l] - w[a] * row
        full = []
        for a in range(tiles):
            root = lax.rsqrt(piv[a])
            out = [v * root for v in M_[a]]
            ident = out.pop()
            at = ln + home * 128
            out[home] = jnp.where((at >= r0) & (at < r0 + b), ident, out[home])
            full.append(jnp.concatenate(out, axis=1))
        U = jnp.concatenate(full, axis=0)
        done.append(U)
        if p + 1 < n // b:
            r1 = r0 + b
            cut = r1 // 128 * 128
            upd = dot(U[:, cut:], U, 0, 0, HI)
            for q in range(p + 1, n // b):
                old = jnp.where((lanes >= r0) & (lanes < r1), 0.0, panels[q])
                panels[q] = old - upd[q * b - cut:(q + 1) * b - cut, :]
    W = jnp.concatenate(done, axis=0)
    li = lax.broadcasted_iota(jnp.int32, (n, n), 1)
    si = lax.broadcasted_iota(jnp.int32, (n, n), 0)
    return jnp.where(li <= si, W, 0.0)


class Place:
    def __init__(self, ssem, rsem):
        self.ssem, self.rsem = ssem, rsem
        self.sends = []
        self.f = lax.axis_index("fsdp")
        self.t = lax.axis_index("tp")
        self.core = lax.rem(self.f, 2)
        self.other = 1 - self.core
        self.x = lax.rem(self.f // 2, NX)
        self.y = self.f // (2 * NX)
        self.xs = [lax.rem(self.x + j, NX) for j in range(NX)]
        self.ys = [lax.rem(self.y + j, NY) for j in range(NY)]
        self.zs = [lax.rem(self.t + j, NZ) for j in range(NZ)]
        self.sibling = self.dev(self.x, self.y, self.other)
        self.zdev = [(self.f, z) for z in self.zs]
        self.all = [lax.rem(self.f + j, NF) for j in range(NF)]
        self.fdev = [(g, self.t) for g in self.all]
        self.plane = [
            self.dev(self.xs[i], self.ys[j], self.core) for i in range(NX) for j in range(NY) if (i, j) != (0, 0)
        ]
        self.chips = [self.ys[j] * NX + self.xs[i] for i in range(NX) for j in range(NY) if (i, j) != (0, 0)]
        self.chip = self.y * NX + self.x
        self.ways = (
            (self.xs, self.dev(self.xs[1], self.y, self.core), self.dev(self.xs[3], self.y, self.core)),
            (self.ys, self.dev(self.x, self.ys[1], self.core), self.dev(self.x, self.ys[3], self.core)),
        )

    def dev(self, px, py, pc):
        return ((py * NX + px) * 2 + pc, self.t)

    def greet(self, devices):
        barrier = pltpu.get_barrier_semaphore()
        for device in devices:
            pl.semaphore_signal(barrier, inc=1, device_id=device, device_id_type=MESH)
        return lambda: pl.semaphore_wait(barrier, len(devices))

    def exchange(self, src, dst, device):
        k = len(self.sends)
        cp = pltpu.make_async_remote_copy(
            src_ref=src, dst_ref=dst, send_sem=self.ssem.at[k], recv_sem=self.rsem.at[k],
            device_id=device, device_id_type=MESH,
        )
        cp.start()
        self.sends.append(cp)
        return cp

    def share(self, ref, device):
        return self.exchange(ref, ref, device)

    def finish(self):
        for cp in self.sends:
            cp.wait_send()


def piece(z, size):
    return pl.ds(pl.multiple_of(z * size, size), size)


def step_kernel(g_hbm, m_hbm, b_hbm, out, both, inverse, gbuf, mbuf, bbuf, bht, part, rz, left, gpart, rg, own, r2, gram,
                r, rc, r16, f1, sab, f2, sq, qc, qp, qz, load, ssem, rsem):
    at = Place(ssem, rsem)
    core, other, x, y, xs, ys = at.core, at.other, at.x, at.y, at.xs, at.ys
    nc = COLS // CHUNK
    loads = []
    for c in range(nc):
        cols = pl.ds(c * CHUNK, CHUNK)
        three = [
            pltpu.make_async_copy(b_hbm.at[cols, :], bbuf.at[cols, :], load.at[3 * c]),
            pltpu.make_async_copy(g_hbm.at[:, cols], gbuf.at[:, cols], load.at[3 * c + 1]),
            pltpu.make_async_copy(m_hbm.at[:, cols], mbuf.at[:, cols], load.at[3 * c + 2]),
        ]
        for cp in three:
            cp.start()
        loads.append(three)
    ready = at.greet(at.zdev[1:] + at.fdev[1:])
    total = None
    for c in range(nc):
        for cp in loads[c]:
            cp.wait()
        cols = pl.ds(c * CHUNK, CHUNK)
        half = (mbuf[:, cols].astype(F32) + gbuf[:, cols].astype(F32)).astype(BF16)
        gbuf[:, cols] = half
        term = dot(half, bbuf[cols, :], 1, 0)
        total = term if c == 0 else total + term
    part[...] = (total * (1.0 / math.sqrt(N))).astype(BF16)
    ready()
    zr = ROWS // NZ
    cps = [at.exchange(part.at[piece(at.zs[j], zr), :], rz.at[j - 1], at.zdev[j]) for j in range(1, NZ)]
    for c in range(nc):
        cols = pl.ds(c * CHUNK, CHUNK)
        bht[cols, :] = gbuf[:, cols].T
    mine = part[piece(at.t, zr), :].astype(F32)
    for j in range(1, NZ):
        cps[j - 1].wait_recv()
        mine = mine + rz[j - 1].astype(F32)
    mine = mine.astype(BF16)
    left[piece(at.t, zr), :] = mine
    az = [at.share(left.at[piece(at.t, zr), :], at.zdev[j]) for j in range(1, NZ)]

    gr = RANK // NF
    gpart[...] = dot(mine, mine, 0, 0)
    cps = [at.exchange(gpart.at[piece(at.all[j], gr), :], rg.at[j - 1], at.fdev[j]) for j in range(1, NF)]
    acc = gpart[piece(at.f, gr), :]
    for j in range(1, NF):
        cps[j - 1].wait_recv()
        acc = acc + rg[j - 1]
    own[...] = acc
    cps = [at.exchange(own, r2.at[j - 1], at.zdev[j]) for j in range(1, NZ)]

    for cp in az:
        cp.wait_recv()
    wide = COLS // 2
    nk = wide // CHUNK
    qk = NX // nk

    def product(k, pc):
        half = bht[pl.ds(pl.multiple_of(pc * wide + k * CHUNK, 128), CHUNK), :]
        val = dot(half, left[...], 1, 0)
        for h in range(2):
            r[h, pc, k * qk:(k + 1) * qk] = val[:, 128 * h:128 * h + 128].reshape(qk, NY, BLOCK, 128)

    cc = []
    for k in range(nk):
        product(k, other)
        qs = pl.ds(k * qk, qk)
        cc.append([at.exchange(r.at[h, other, qs], rc.at[h, qs], at.sibling) for h in range(2)])
    for j in range(1, NZ):
        cps[j - 1].wait_recv()
        acc = acc + r2[j - 1]
    grow = piece(at.f, gr)
    gram[grow, :] = acc
    ga = [at.share(gram.at[grow, :], at.fdev[j]) for j in range(1, NF)]
    for k in range(nk):
        product(k, core)
    for k in range(nk):
        qs = pl.ds(k * qk, qk)
        for h in range(2):
            cc[k][h].wait_recv()
            total = r[h, core, qs] + rc[h, qs]
            r[h, core, qs] = total
            r16[h, qs] = total.astype(BF16)
    one = [[], []]
    for j in range(1, NX):
        one[0].append(at.exchange(r16.at[0, xs[j]], f1.at[0, j - 1], at.dev(xs[j], y, core)))
        one[1].append(at.exchange(r16.at[1, :, ys[j]], f1.at[1, j - 1], at.dev(x, ys[j], core)))
    for cp in ga:
        cp.wait_recv()
    w = lower_inverse(gram[...])
    two = [[], []]
    for h in range(2):
        total = r[0, core, x] if h == 0 else r[1, core, :, y]
        for j in range(1, NX):
            one[h][j - 1].wait_recv()
            total = total + f1[h, j - 1].astype(F32)
        sab[h] = total
        for j in range(1, NX):
            if h == 0:
                two[h].append(at.exchange(sab.at[h, ys[j]], f2.at[h, j - 1], at.dev(x, ys[j], core)))
            else:
                two[h].append(at.exchange(sab.at[h, xs[j]], f2.at[h, j - 1], at.dev(xs[j], y, core)))
    ortho = dot(left[...].astype(F32), w, 1, 1, HI)
    both[0:ROWS, :] = ortho.astype(BF16)
    halves = []
    for h in range(2):
        total = sab[h, y if h == 0 else x]
        for j in range(1, NX):
            two[h][j - 1].wait_recv()
            total = total + f2[h, j - 1]
        halves.append(total)
    right = dot(jnp.concatenate(halves, axis=1), w, 1, 1, HI)
    rounded = right.astype(BF16)
    for h in range(2):
        out[h, core, x, y] = rounded[:, 128 * h:128 * h + 128]
    g2 = []
    for j in range(1, NX):
        g2.append(at.share(out.at[0, core, x, y], at.dev(x, ys[j], core)))
        g2.append(at.share(out.at[1, core, x, y], at.dev(xs[j], y, core)))
    total = jnp.sum(right * right, axis=0, keepdims=True)
    srow = lax.broadcasted_iota(jnp.int32, (8, 128), 0)
    sq[...] = jnp.where(srow == 0, total[:, :128], total[:, 128:])
    sc = at.exchange(sq, qc, at.sibling)
    sc.wait_recv()
    qp[at.chip] = sq[...] + qc[...]
    sp = [at.share(qp.at[at.chip], device) for device in at.plane]
    for cp in g2:
        cp.wait_recv()

    def band(h, q, k=None):
        if k is None:
            return out.at[0, core, q] if h == 0 else out.at[1, core, :, q]
        return out.at[0, core, q, pl.ds(2 * k, 2)] if h == 0 else out.at[1, core, pl.ds(2 * k, 2), q]

    begun = []
    for h in range(2):
        pos, nxt, prv = at.ways[h]
        begun.append([at.share(band(h, pos[0], 0), nxt), at.share(band(h, pos[0], 1), prv)])
    for h in range(2):
        pos, nxt, prv = at.ways[h]
        begun[h] += [at.share(band(h, pos[0], 1), nxt), at.share(band(h, pos[0], 0), prv)]
    last = [at.share(band(h, at.ways[h][0][0]), at.sibling) for h in range(2)]
    for cp in sp:
        cp.wait_recv()
    total = qp[0]
    for j in range(1, NX * NY):
        total = total + qp[j]
    qz[at.t] = total
    sz = [at.share(qz.at[at.t], at.zdev[j]) for j in range(1, NZ)]
    relays = []
    for h in range(2):
        pos, nxt, prv = at.ways[h]
        begun[h][0].wait_recv()
        relays.append(at.share(band(h, pos[3], 0), nxt))
        begun[h][1].wait_recv()
        relays.append(at.share(band(h, pos[1], 1), prv))
    for cp in sz:
        cp.wait_recv()
    total = qz[0]
    for j in range(1, NZ):
        total = total + qz[j]
    scale = jnp.sqrt(jnp.concatenate([total[0:1, :], total[1:2, :]], axis=1) / N + 1e-06)
    inverse[...] = jnp.broadcast_to(1.0 / scale, (8, RANK))
    both[ROWS:, :] = (ortho * (math.sqrt(M / RANK) / scale)).astype(BF16)
    for h in range(2):
        pos = at.ways[h][0]
        begun[h][2].wait_recv()
        last.append(at.share(band(h, pos[3]), at.sibling))
        begun[h][3].wait_recv()
        last.append(at.share(band(h, pos[1]), at.sibling))
    for h in range(2):
        pos = at.ways[h][0]
        for k in range(2):
            relays[2 * h + k].wait_recv()
            last.append(at.share(band(h, pos[2], k), at.sibling))
    for cp in last:
        cp.wait_recv()
    at.finish()


def output_kernel(g, m, both, right, inverse, update, new_momentum, new_basis):
    rr = jnp.concatenate([right[0], right[1]], axis=1)
    product = dot(both[...], rr, 1, 1)
    buffer = m[...].astype(F32) + g[...].astype(F32)
    new_momentum[...] = (buffer - (1.0 - MU / 100.0) * product[:ROWS]).astype(BF16)
    update[...] = product[ROWS:].astype(BF16)
    new_basis[...] = (rr.astype(F32) * inverse[0:1, :]).astype(BF16)


def body(grad, momentum, basis):
    dma = pltpu.SemaphoreType.DMA
    zr = ROWS // NZ
    gr = RANK // NF
    sends = 7 + 7 + 31 + 7 + 31 + 4 + 6 + 6 + 6 + 1 + 15 + 8 + 2 + 7 + 4 + 8
    right, both, inverse = pl.pallas_call(
        step_kernel,
        out_shape=(
            jax.ShapeDtypeStruct((2, 2, NX, NY, BLOCK, 128), BF16),
            jax.ShapeDtypeStruct((2 * ROWS, RANK), BF16),
            jax.ShapeDtypeStruct((8, RANK), F32),
        ),
        in_specs=[pl.BlockSpec(memory_space=pl.ANY)] * 3,
        out_specs=tuple(pl.BlockSpec(memory_space=pltpu.VMEM) for _ in range(3)),
        scratch_shapes=[
            pltpu.VMEM((ROWS, COLS), BF16), pltpu.VMEM((ROWS, COLS), BF16), pltpu.VMEM((COLS, RANK), BF16),
            pltpu.VMEM((COLS, RANK), BF16),
            pltpu.VMEM((ROWS, RANK), BF16), pltpu.VMEM((NZ - 1, zr, RANK), BF16), pltpu.VMEM((ROWS, RANK), BF16),
            pltpu.VMEM((RANK, RANK), F32), pltpu.VMEM((NF - 1, gr, RANK), F32),
            pltpu.VMEM((gr, RANK), F32), pltpu.VMEM((NZ - 1, gr, RANK), F32), pltpu.VMEM((RANK, RANK), F32),
            pltpu.VMEM((2, 2, NX, NY, BLOCK, 128), F32), pltpu.VMEM((2, NX, NY, BLOCK, 128), F32),
            pltpu.VMEM((2, NX, NY, BLOCK, 128), BF16), pltpu.VMEM((2, 3, 4, BLOCK, 128), BF16),
            pltpu.VMEM((2, 4, BLOCK, 128), F32), pltpu.VMEM((2, 3, BLOCK, 128), F32),
            pltpu.VMEM((8, 128), F32), pltpu.VMEM((8, 128), F32),
            pltpu.VMEM((NX * NY, 8, 128), F32), pltpu.VMEM((NZ, 8, 128), F32),
            dma((3 * (COLS // CHUNK),)), dma((sends,)), dma((sends,)),
        ],
        compiler_params=pltpu.CompilerParams(collective_id=0, has_side_effects=True, vmem_limit_bytes=VMEM_LIMIT),
        name="step_kernel",
    )(grad, momentum, basis)
    step = 512
    return pl.pallas_call(
        output_kernel,
        grid=(COLS // step,),
        out_shape=(
            jax.ShapeDtypeStruct((ROWS, COLS), BF16),
            jax.ShapeDtypeStruct((ROWS, COLS), BF16),
            jax.ShapeDtypeStruct((COLS, RANK), BF16),
        ),
        in_specs=[
            pl.BlockSpec((ROWS, step), lambda i: (0, i)),
            pl.BlockSpec((ROWS, step), lambda i: (0, i)),
            pl.BlockSpec((2 * ROWS, RANK), lambda i: (0, 0)),
            pl.BlockSpec((2, step, 128), lambda i: (0, i, 0)),
            pl.BlockSpec((8, RANK), lambda i: (0, 0)),
        ],
        out_specs=(
            pl.BlockSpec((ROWS, step), lambda i: (0, i)),
            pl.BlockSpec((ROWS, step), lambda i: (0, i)),
            pl.BlockSpec((step, RANK), lambda i: (i, 0)),
        ),
        compiler_params=pltpu.CompilerParams(vmem_limit_bytes=VMEM_LIMIT),
        name="output_kernel",
    )(grad, momentum, both, right.reshape(2, COLS, 128), inverse)


def solution(mesh):
    placed = (P("fsdp", "tp"), P("fsdp", "tp"), P("tp", None))
    return jax.shard_map(
        body,
        mesh=mesh,
        in_specs=placed,
        out_specs=(P("fsdp", "tp"), P("fsdp", "tp"), P("tp", None)),
        check_vma=False,
    )
```

time: 425 us -> 76.8 us (0.18)
  waiting for transfers between devices: 309 us -> 0 us
  Pallas kernels: 0 us -> 76 us
  other arithmetic: 59.7 us -> 0 us
  matrix products: 16 us -> 0 us
  between operations: 15.2 us -> 0.64 us
  blocking collectives: 13.7 us -> 0 us
  local copies, waits for them, and re-layouts: 7.23 us -> 0 us
    psum x3 -> x0, waiting for transfers between devices: 308 us -> none  [the longest x1 121 us: body(): right = lax.psum(partial_right, 'fsdp')]
    pallas_call x0 -> x2, Pallas kernels: none -> 76 us  [the longest x1 67.7 us: body(): pl.pallas_call(step_kernel, out_shape=(jax.ShapeDtypeStruct((2, 2, NX, NY...]
    another operation x9 -> x0, other arithmetic: 53.7 us -> none  [the longest x6 34 us: orthonormal(): lower = jnp.linalg.cholesky(gram)]
    dot_general x5 -> x0, matrix products: 14.5 us -> none  [the longest x1 4.58 us: body(): lax.dot_general(buffer_half, ortho, (((0,), (0,)), ((), ())), preferred_e...]
    psum x1 -> x0, blocking collectives: 13.7 us -> none  [body(): squares = lax.psum(jnp.sum(right * right, axis=0), 'tp')]
  transfers between devices with their start and end apart: 3 -> 0, of which waited for: 3 -> 0; matrix products, arithmetic and copies ran while one was open for 0% -> 0% of each run, Pallas kernels for 0% -> 0%
where the time goes in v4:
time: 76.8 us; the launch traced here: 76.6 us
  Pallas kernels  76 us (99%)
    pallas_call x1, Pallas kernels, body(): pl.pallas_call(step_kernel, out_shape=(jax.ShapeDtypeStruct((2, 2, NX, NY...  67.7 us
    pallas_call x1, Pallas kernels, body(): pl.pallas_call(output_kernel, grid=(COLS // step,), out_shape=(jax.ShapeD...  8.24 us

profile of v4, /device:TPU:1, one launch (start us, length us, event | category | flops | bytes accessed | tf_op | source)
XLA Modules:
  0.0 76.6 jit_solution(3789858298925288623)
XLA Ops:
  0.6 67.7 %step_kernel.1 = (bf16[2,2,4,4,112,128]{5,4,3,2,1,0:T(8,128)(2,1)}, bf16[512,256]{1,0:T(8,128)(2,1)}, f32[8,256]{1,0:T(8,128)}) custom-call(bf16[256,3584]{1,0:T(8,128)(2,1)} %g.1, bf16[256,3584]{1,0:T(8,128)(2,1)} %m.1, bf16[3584,256]{1,0:T(8,128)(2,1)} %b_hbm.1), custom_call_target="tpu_custom_call" | custom-call | tf_op jit(solution)/shard_map/step_kernel/pallas_call | solution.py:348
  68.3 8.2 %output_kernel.1 = (bf16[256,3584]{1,0:T(8,128)(2,1)}, bf16[256,3584]{1,0:T(8,128)(2,1)}, bf16[3584,256]{1,0:T(8,128)(2,1)}) custom-call(bf16[256,3584]{1,0:T(8,128)(2,1)} %g.1, bf16[256,3584]{1,0:T(8,128)(2,1)} %m.1, bf16[512,256]{1,0:T(8,128)(2,1)} %get-tuple-element.6.both, bf16[2,3584,128]{2,1,0:T(8,128)(2,1)} %bitcast.1, f32[8,256]{1,0:T(8,128)} %get-tuple-element.8.inverse), custom_call_target="tpu_custom_call" | custom-call | tf_op jit(solution)/shard_map/output_kernel/pallas_call | solution.py:374

commit v5 on v4

--- a/solution.py
+++ b/solution.py
@@ -22,6 +22,7 @@
 COLS = N // NZ
 CHUNK = 896
 BLOCK = COLS // NF
+STEP = 512
 VMEM_LIMIT = 60 * 1024 * 1024
 
 
@@ -31,7 +32,16 @@
     )
 
 
-def lower_inverse(gram, b=64, s8=8):
+def lane_of(tile, j):
+    return jnp.broadcast_to(tile[j:j + 1, :], tile.shape)
+
+
+def reciprocal(v):
+    near = pl.reciprocal(v, approx=True)
+    return near * (2.0 - v * near)
+
+
+def lower_inverse(gram, beside, b=64, s8=8):
     n = gram.shape[0]
     tiles = b // 8
     nt = n // 128
@@ -55,21 +65,30 @@
                 C.append([
                     jnp.broadcast_to(M_[a][home][:, lane:lane + 1], (8, 128)) if a >= s else None for a in range(tiles)
                 ])
-            for j in range(s8):
-                sj = jnp.broadcast_to(C[j][s][j:j + 1, :], (8, 128))
-                near = pl.reciprocal(sj, approx=True)
-                inv = near * (2.0 - sj * near)
-                w = [C[j][a] * inv if a >= s else None for a in range(tiles)]
-                for k in range(j + 1, s8):
-                    bk = jnp.broadcast_to(C[j][s][k:k + 1, :], (8, 128))
+            for j in range(0, s8, 2):
+                first, second = C[j], C[j + 1]
+                p11 = lane_of(first[s], j)
+                p12 = lane_of(first[s], j + 1)
+                p22 = lane_of(second[s], j + 1)
+                det = p11 * p22 - p12 * p12
+                inv1 = reciprocal(p11)
+                mult = p12 * inv1
+                inv2 = p11 * reciprocal(det)
+                w1 = [first[a] * inv1 if a >= s else None for a in range(tiles)]
+                w2 = [(second[a] - first[a] * mult) * inv2 if a >= s else None for a in range(tiles)]
+                for k in range(j + 2, s8):
+                    b1 = lane_of(first[s], k)
+                    b2 = lane_of(second[s], k) - b1 * mult
                     for a in range(s, tiles):
-                        C[k][a] = C[k][a] - w[a] * bk
-                w[s] = jnp.where(rows > j, w[s], 0.0)
-                piv[s] = jnp.where(rows == j, sj, piv[s])
+                        C[k][a] = (C[k][a] - w1[a] * b1) - w2[a] * b2
+                w1[s] = jnp.where(rows > j, w1[s], 0.0)
+                w2[s] = jnp.where(rows > j + 1, w2[s], 0.0)
+                piv[s] = jnp.where(rows == j, p11, jnp.where(rows == j + 1, det * inv1, piv[s]))
                 for l in range(nt + 1):
-                    row = jnp.broadcast_to(M_[s][l][j:j + 1, :], (8, 128))
+                    b1 = lane_of(M_[s][l], j)
+                    b2 = lane_of(M_[s][l], j + 1) - b1 * mult
                     for a in range(s, tiles):
-                        M_[a][l] = M_[a][l] - w[a] * row
+                        M_[a][l] = (M_[a][l] - w1[a] * b1) - w2[a] * b2
         full = []
         for a in range(tiles):
             root = lax.rsqrt(piv[a])
@@ -87,6 +106,8 @@
             for q in range(p + 1, n // b):
                 old = jnp.where((lanes >= r0) & (lanes < r1), 0.0, panels[q])
                 panels[q] = old - upd[q * b - cut:(q + 1) * b - cut, :]
+            if p in beside:
+                beside[p]()
     W = jnp.concatenate(done, axis=0)
     li = lax.broadcasted_iota(jnp.int32, (n, n), 1)
     si = lax.broadcasted_iota(jnp.int32, (n, n), 0)
@@ -240,19 +261,22 @@
         one[1].append(at.exchange(r16.at[1, :, ys[j]], f1.at[1, j - 1], at.dev(x, ys[j], core)))
     for cp in ga:
         cp.wait_recv()
-    w = lower_inverse(gram[...])
     two = [[], []]
-    for h in range(2):
-        total = r[0, core, x] if h == 0 else r[1, core, :, y]
-        for j in range(1, NX):
-            one[h][j - 1].wait_recv()
-            total = total + f1[h, j - 1].astype(F32)
-        sab[h] = total
-        for j in range(1, NX):
-            if h == 0:
-                two[h].append(at.exchange(sab.at[h, ys[j]], f2.at[h, j - 1], at.dev(x, ys[j], core)))
-            else:
-                two[h].append(at.exchange(sab.at[h, xs[j]], f2.at[h, j - 1], at.dev(xs[j], y, core)))
+
+    def second_stage():
+        for h in range(2):
+            total = r[0, core, x] if h == 0 else r[1, core, :, y]
+            for j in range(1, NX):
+                one[h][j - 1].wait_recv()
+                total = total + f1[h, j - 1].astype(F32)
+            sab[h] = total
+            for j in range(1, NX):
+                if h == 0:
+                    two[h].append(at.exchange(sab.at[h, ys[j]], f2.at[h, j - 1], at.dev(x, ys[j], core)))
+                else:
+                    two[h].append(at.exchange(sab.at[h, xs[j]], f2.at[h, j - 1], at.dev(xs[j], y, core)))
+
+    w = lower_inverse(gram[...], {2: second_stage})
     ortho = dot(left[...].astype(F32), w, 1, 1, HI)
     both[0:ROWS, :] = ortho.astype(BF16)
     halves = []
@@ -331,13 +355,50 @@
     at.finish()
 
 
-def output_kernel(g, m, both, right, inverse, update, new_momentum, new_basis):
-    rr = jnp.concatenate([right[0], right[1]], axis=1)
-    product = dot(both[...], rr, 1, 1)
-    buffer = m[...].astype(F32) + g[...].astype(F32)
-    new_momentum[...] = (buffer - (1.0 - MU / 100.0) * product[:ROWS]).astype(BF16)
-    update[...] = product[ROWS:].astype(BF16)
-    new_basis[...] = (rr.astype(F32) * inverse[0:1, :]).astype(BF16)
+def output_kernel(g_hbm, m_hbm, both_hbm, right_hbm, inv_hbm, update, new_momentum, new_basis,
+                  gbuf, mbuf, both, rbuf, inv, ubuf, nbuf, bbuf, load, store):
+    nc = COLS // STEP
+    first = [
+        pltpu.make_async_copy(both_hbm, both, load.at[4 * nc]),
+        pltpu.make_async_copy(inv_hbm, inv, load.at[4 * nc + 1]),
+    ]
+    loads = []
+    for c in range(nc):
+        cols = pl.ds(c * STEP, STEP)
+        loads.append([
+            pltpu.make_async_copy(right_hbm.at[0, cols, :], rbuf.at[0, cols, :], load.at[4 * c]),
+            pltpu.make_async_copy(right_hbm.at[1, cols, :], rbuf.at[1, cols, :], load.at[4 * c + 1]),
+            pltpu.make_async_copy(g_hbm.at[:, cols], gbuf.at[:, cols], load.at[4 * c + 2]),
+            pltpu.make_async_copy(m_hbm.at[:, cols], mbuf.at[:, cols], load.at[4 * c + 3]),
+        ])
+    for cp in first:
+        cp.start()
+    for group in loads:
+        for cp in group:
+            cp.start()
+    for cp in first:
+        cp.wait()
+    stores = []
+    for c in range(nc):
+        cols = pl.ds(c * STEP, STEP)
+        for cp in loads[c]:
+            cp.wait()
+        rr = jnp.concatenate([rbuf[0, cols, :], rbuf[1, cols, :]], axis=1)
+        bbuf[cols, :] = (rr.astype(F32) * inv[0:1, :]).astype(BF16)
+        product = dot(both[...], rr, 1, 1)
+        ubuf[:, cols] = product[ROWS:].astype(BF16)
+        buffer = mbuf[:, cols].astype(F32) + gbuf[:, cols].astype(F32)
+        nbuf[:, cols] = (buffer - (1.0 - MU / 100.0) * product[:ROWS]).astype(BF16)
+        three = [
+            pltpu.make_async_copy(bbuf.at[cols, :], new_basis.at[cols, :], store.at[3 * c]),
+            pltpu.make_async_copy(ubuf.at[:, cols], update.at[:, cols], store.at[3 * c + 1]),
+            pltpu.make_async_copy(nbuf.at[:, cols], new_momentum.at[:, cols], store.at[3 * c + 2]),
+        ]
+        for cp in three:
+            cp.start()
+        stores += three
+    for cp in stores:
+        cp.wait()
 
 
 def body(grad, momentum, basis):
@@ -370,27 +431,22 @@
         compiler_params=pltpu.CompilerParams(collective_id=0, has_side_effects=True, vmem_limit_bytes=VMEM_LIMIT),
         name="step_kernel",
     )(grad, momentum, basis)
-    step = 512
+    nc = COLS // STEP
+    wide = pltpu.VMEM((ROWS, COLS), BF16)
     return pl.pallas_call(
         output_kernel,
-        grid=(COLS // step,),
         out_shape=(
             jax.ShapeDtypeStruct((ROWS, COLS), BF16),
             jax.ShapeDtypeStruct((ROWS, COLS), BF16),
             jax.ShapeDtypeStruct((COLS, RANK), BF16),
         ),
-        in_specs=[
-            pl.BlockSpec((ROWS, step), lambda i: (0, i)),
-            pl.BlockSpec((ROWS, step), lambda i: (0, i)),
-            pl.BlockSpec((2 * ROWS, RANK), lambda i: (0, 0)),
-            pl.BlockSpec((2, step, 128), lambda i: (0, i, 0)),
-            pl.BlockSpec((8, RANK), lambda i: (0, 0)),
+        in_specs=[pl.BlockSpec(memory_space=pl.ANY)] * 5,
+        out_specs=tuple(pl.BlockSpec(memory_space=pl.ANY) for _ in range(3)),
+        scratch_shapes=[
+            wide, wide, pltpu.VMEM((2 * ROWS, RANK), BF16), pltpu.VMEM((2, COLS, 128), BF16), pltpu.VMEM((8, RANK), F32),
+            wide, wide, pltpu.VMEM((COLS, RANK), BF16),
+            dma((4 * nc + 2,)), dma((3 * nc,)),
         ],
-        out_specs=(
-            pl.BlockSpec((ROWS, step), lambda i: (0, i)),
-            pl.BlockSpec((ROWS, step), lambda i: (0, i)),
-            pl.BlockSpec((step, RANK), lambda i: (i, 0)),
-        ),
         compiler_params=pltpu.CompilerParams(vmem_limit_bytes=VMEM_LIMIT),
         name="output_kernel",
     )(grad, momentum, both, right.reshape(2, COLS, 128), inverse)

time: 76.8 us -> 72.8 us (0.948)
  Pallas kernels: 76 us -> 72 us
    pallas_call x1, Pallas kernels: 8.24 us -> 5.11 us  [body(): pl.pallas_call(output_kernel, out_shape=(jax.ShapeDtypeStruct((ROWS, COLS...]
    pallas_call x1, Pallas kernels: 67.7 us -> 66.9 us  [body(): pl.pallas_call(step_kernel, out_shape=(jax.ShapeDtypeStruct((2, 2, NX, NY...]
where the time goes in v5:
time: 72.8 us; the launch traced here: 72.7 us
  Pallas kernels  72 us (99%)
    pallas_call x1, Pallas kernels, body(): pl.pallas_call(step_kernel, out_shape=(jax.ShapeDtypeStruct((2, 2, NX, NY...  66.9 us
    pallas_call x1, Pallas kernels, body(): pl.pallas_call(output_kernel, out_shape=(jax.ShapeDtypeStruct((ROWS, COLS...  5.11 us

profile of v5, /device:TPU:1, one launch (start us, length us, event | category | flops | bytes accessed | tf_op | source)
XLA Modules:
  0.0 72.7 jit_solution(1808076390611065516)
XLA Ops:
  0.6 66.9 %step_kernel.1 = (bf16[2,2,4,4,112,128]{5,4,3,2,1,0:T(8,128)(2,1)}, bf16[512,256]{1,0:T(8,128)(2,1)}, f32[8,256]{1,0:T(8,128)}) custom-call(bf16[256,3584]{1,0:T(8,128)(2,1)} %g_hbm.3, bf16[256,3584]{1,0:T(8,128)(2,1)} %m_hbm.3, bf16[3584,256]{1,0:T(8,128)(2,1)} %b_hbm.1), custom_call_target="tpu_custom_call" | custom-call | tf_op jit(solution)/shard_map/step_kernel/pallas_call | solution.py:409
  67.6 5.1 %output_kernel.1 = (bf16[256,3584]{1,0:T(8,128)(2,1)}, bf16[256,3584]{1,0:T(8,128)(2,1)}, bf16[3584,256]{1,0:T(8,128)(2,1)}) custom-call(bf16[256,3584]{1,0:T(8,128)(2,1)} %g_hbm.3, bf16[256,3584]{1,0:T(8,128)(2,1)} %m_hbm.3, bf16[512,256]{1,0:T(8,128)(2,1)} %get-tuple-element.6.both_hbm, bf16[2,3584,128]{2,1,0:T(8,128)(2,1)} %bitcast.1, ...), custom_call_target="tpu_custom_call" | custom-call | tf_op jit(solution)/shard_map/output_kernel/pallas_call | solution.py:436

commit v6 on v5

--- a/solution.py
+++ b/solution.py
@@ -172,14 +172,14 @@
     return pl.ds(pl.multiple_of(z * size, size), size)
 
 
-def step_kernel(g_hbm, m_hbm, b_hbm, out, both, inverse, gbuf, mbuf, bbuf, bht, part, rz, left, gpart, rg, own, r2, gram,
-                r, rc, r16, f1, sab, f2, sq, qc, qp, qz, load, ssem, rsem):
+def step_kernel(g_hbm, m_hbm, b_hbm, result, both, inverse, gbuf, mbuf, bbuf, bht, part, rz, left, gpart, rg, own, r2, gram,
+                out, rs, r, rc, r16, f1, sab, s16, f2, sq, qc, qp, qz, load, store, ssem, rsem):
     at = Place(ssem, rsem)
     core, other, x, y, xs, ys = at.core, at.other, at.x, at.y, at.xs, at.ys
-    nc = COLS // CHUNK
+    nc = COLS // STEP
     loads = []
     for c in range(nc):
-        cols = pl.ds(c * CHUNK, CHUNK)
+        cols = pl.ds(c * STEP, STEP)
         three = [
             pltpu.make_async_copy(b_hbm.at[cols, :], bbuf.at[cols, :], load.at[3 * c]),
             pltpu.make_async_copy(g_hbm.at[:, cols], gbuf.at[:, cols], load.at[3 * c + 1]),
@@ -193,7 +193,7 @@
     for c in range(nc):
         for cp in loads[c]:
             cp.wait()
-        cols = pl.ds(c * CHUNK, CHUNK)
+        cols = pl.ds(c * STEP, STEP)
         half = (mbuf[:, cols].astype(F32) + gbuf[:, cols].astype(F32)).astype(BF16)
         gbuf[:, cols] = half
         term = dot(half, bbuf[cols, :], 1, 0)
@@ -203,7 +203,7 @@
     zr = ROWS // NZ
     cps = [at.exchange(part.at[piece(at.zs[j], zr), :], rz.at[j - 1], at.zdev[j]) for j in range(1, NZ)]
     for c in range(nc):
-        cols = pl.ds(c * CHUNK, CHUNK)
+        cols = pl.ds(c * STEP, STEP)
         bht[cols, :] = gbuf[:, cols].T
     mine = part[piece(at.t, zr), :].astype(F32)
     for j in range(1, NZ):
@@ -229,17 +229,17 @@
     nk = wide // CHUNK
     qk = NX // nk
 
-    def product(k, pc):
+    def product(k, pc, into):
         half = bht[pl.ds(pl.multiple_of(pc * wide + k * CHUNK, 128), CHUNK), :]
         val = dot(half, left[...], 1, 0)
         for h in range(2):
-            r[h, pc, k * qk:(k + 1) * qk] = val[:, 128 * h:128 * h + 128].reshape(qk, NY, BLOCK, 128)
+            into[h, k * qk:(k + 1) * qk] = val[:, 128 * h:128 * h + 128].reshape(qk, NY, BLOCK, 128).astype(into.dtype)
 
     cc = []
     for k in range(nk):
-        product(k, other)
+        product(k, other, rs)
         qs = pl.ds(k * qk, qk)
-        cc.append([at.exchange(r.at[h, other, qs], rc.at[h, qs], at.sibling) for h in range(2)])
+        cc.append([at.exchange(rs.at[h, qs], rc.at[h, qs], at.sibling) for h in range(2)])
     for j in range(1, NZ):
         cps[j - 1].wait_recv()
         acc = acc + r2[j - 1]
@@ -247,13 +247,13 @@
     gram[grow, :] = acc
     ga = [at.share(gram.at[grow, :], at.fdev[j]) for j in range(1, NF)]
     for k in range(nk):
-        product(k, core)
+        product(k, core, r)
     for k in range(nk):
         qs = pl.ds(k * qk, qk)
         for h in range(2):
             cc[k][h].wait_recv()
-            total = r[h, core, qs] + rc[h, qs]
-            r[h, core, qs] = total
+            total = r[h, qs] + rc[h, qs].astype(F32)
+            r[h, qs] = total
             r16[h, qs] = total.astype(BF16)
     one = [[], []]
     for j in range(1, NX):
@@ -265,16 +265,17 @@
 
     def second_stage():
         for h in range(2):
-            total = r[0, core, x] if h == 0 else r[1, core, :, y]
+            total = r[0, x] if h == 0 else r[1, :, y]
             for j in range(1, NX):
                 one[h][j - 1].wait_recv()
                 total = total + f1[h, j - 1].astype(F32)
             sab[h] = total
+            s16[h] = total.astype(BF16)
             for j in range(1, NX):
                 if h == 0:
-                    two[h].append(at.exchange(sab.at[h, ys[j]], f2.at[h, j - 1], at.dev(x, ys[j], core)))
+                    two[h].append(at.exchange(s16.at[h, ys[j]], f2.at[h, j - 1], at.dev(x, ys[j], core)))
                 else:
-                    two[h].append(at.exchange(sab.at[h, xs[j]], f2.at[h, j - 1], at.dev(xs[j], y, core)))
+                    two[h].append(at.exchange(s16.at[h, xs[j]], f2.at[h, j - 1], at.dev(xs[j], y, core)))
 
     w = lower_inverse(gram[...], {2: second_stage})
     ortho = dot(left[...].astype(F32), w, 1, 1, HI)
@@ -284,7 +285,7 @@
         total = sab[h, y if h == 0 else x]
         for j in range(1, NX):
             two[h][j - 1].wait_recv()
-            total = total + f2[h, j - 1]
+            total = total + f2[h, j - 1].astype(F32)
         halves.append(total)
     right = dot(jnp.concatenate(halves, axis=1), w, 1, 1, HI)
     rounded = right.astype(BF16)
@@ -304,10 +305,22 @@
     for cp in g2:
         cp.wait_recv()
 
-    def band(h, q, k=None):
+    def band(h, q, k=None, ref=out, pc=core):
         if k is None:
-            return out.at[0, core, q] if h == 0 else out.at[1, core, :, q]
-        return out.at[0, core, q, pl.ds(2 * k, 2)] if h == 0 else out.at[1, core, pl.ds(2 * k, 2), q]
+            return ref.at[0, pc, q] if h == 0 else ref.at[1, pc, :, q]
+        return ref.at[0, pc, q, pl.ds(2 * k, 2)] if h == 0 else ref.at[1, pc, pl.ds(2 * k, 2), q]
+
+    last, spans, stores = [], [], []
+
+    def keep(h, q, k, pc):
+        cp = pltpu.make_async_copy(band(h, q, k, out, pc), band(h, q, k, result, pc), store.at[len(stores)])
+        cp.start()
+        stores.append(cp)
+
+    def forward(h, q, k=None):
+        last.append(at.share(band(h, q, k), at.sibling))
+        spans.append((h, q, k))
+        keep(h, q, k, core)
 
     begun = []
     for h in range(2):
@@ -316,7 +329,8 @@
     for h in range(2):
         pos, nxt, prv = at.ways[h]
         begun[h] += [at.share(band(h, pos[0], 1), nxt), at.share(band(h, pos[0], 0), prv)]
-    last = [at.share(band(h, at.ways[h][0][0]), at.sibling) for h in range(2)]
+    for h in range(2):
+        forward(h, at.ways[h][0][0])
     for cp in sp:
         cp.wait_recv()
     total = qp[0]
@@ -342,17 +356,20 @@
     for h in range(2):
         pos = at.ways[h][0]
         begun[h][2].wait_recv()
-        last.append(at.share(band(h, pos[3]), at.sibling))
+        forward(h, pos[3])
         begun[h][3].wait_recv()
-        last.append(at.share(band(h, pos[1]), at.sibling))
+        forward(h, pos[1])
     for h in range(2):
         pos = at.ways[h][0]
         for k in range(2):
             relays[2 * h + k].wait_recv()
-            last.append(at.share(band(h, pos[2], k), at.sibling))
-    for cp in last:
-        cp.wait_recv()
+            forward(h, pos[2], k)
+    for cp, (h, q, k) in zip(last, spans):
+        cp.wait_recv()
+        keep(h, q, k, other)
     at.finish()
+    for cp in stores:
+        cp.wait()
 
 
 def output_kernel(g_hbm, m_hbm, both_hbm, right_hbm, inv_hbm, update, new_momentum, new_basis,
@@ -414,19 +431,20 @@
             jax.ShapeDtypeStruct((8, RANK), F32),
         ),
         in_specs=[pl.BlockSpec(memory_space=pl.ANY)] * 3,
-        out_specs=tuple(pl.BlockSpec(memory_space=pltpu.VMEM) for _ in range(3)),
+        out_specs=tuple(pl.BlockSpec(memory_space=v) for v in (pl.ANY, pltpu.VMEM, pltpu.VMEM)),
         scratch_shapes=[
             pltpu.VMEM((ROWS, COLS), BF16), pltpu.VMEM((ROWS, COLS), BF16), pltpu.VMEM((COLS, RANK), BF16),
             pltpu.VMEM((COLS, RANK), BF16),
             pltpu.VMEM((ROWS, RANK), BF16), pltpu.VMEM((NZ - 1, zr, RANK), BF16), pltpu.VMEM((ROWS, RANK), BF16),
             pltpu.VMEM((RANK, RANK), F32), pltpu.VMEM((NF - 1, gr, RANK), F32),
             pltpu.VMEM((gr, RANK), F32), pltpu.VMEM((NZ - 1, gr, RANK), F32), pltpu.VMEM((RANK, RANK), F32),
-            pltpu.VMEM((2, 2, NX, NY, BLOCK, 128), F32), pltpu.VMEM((2, NX, NY, BLOCK, 128), F32),
+            pltpu.VMEM((2, 2, NX, NY, BLOCK, 128), BF16), pltpu.VMEM((2, NX, NY, BLOCK, 128), BF16),
+            pltpu.VMEM((2, NX, NY, BLOCK, 128), F32), pltpu.VMEM((2, NX, NY, BLOCK, 128), BF16),
             pltpu.VMEM((2, NX, NY, BLOCK, 128), BF16), pltpu.VMEM((2, 3, 4, BLOCK, 128), BF16),
-            pltpu.VMEM((2, 4, BLOCK, 128), F32), pltpu.VMEM((2, 3, BLOCK, 128), F32),
+            pltpu.VMEM((2, 4, BLOCK, 128), F32), pltpu.VMEM((2, 4, BLOCK, 128), BF16), pltpu.VMEM((2, 3, BLOCK, 128), BF16),
             pltpu.VMEM((8, 128), F32), pltpu.VMEM((8, 128), F32),
             pltpu.VMEM((NX * NY, 8, 128), F32), pltpu.VMEM((NZ, 8, 128), F32),
-            dma((3 * (COLS // CHUNK),)), dma((sends,)), dma((sends,)),
+            dma((3 * (COLS // STEP),)), dma((20,)), dma((sends,)), dma((sends,)),
         ],
         compiler_params=pltpu.CompilerParams(collective_id=0, has_side_effects=True, vmem_limit_bytes=VMEM_LIMIT),
         name="step_kernel",

time: 72.8 us -> 71.6 us (0.984)
  Pallas kernels: 72 us -> 70.9 us
    pallas_call x1, Pallas kernels: 66.9 us -> 65.8 us  [body(): pl.pallas_call(step_kernel, out_shape=(jax.ShapeDtypeStruct((2, 2, NX, NY...]
where the time goes in v6:
time: 71.6 us
  Pallas kernels  70.9 us (99%)
    pallas_call x1, Pallas kernels, body(): pl.pallas_call(step_kernel, out_shape=(jax.ShapeDtypeStruct((2, 2, NX, NY...  65.8 us
    pallas_call x1, Pallas kernels, body(): pl.pallas_call(output_kernel, out_shape=(jax.ShapeDtypeStruct((ROWS, COLS...  5.11 us

profile of v6, /device:TPU:1, one launch (start us, length us, event | category | flops | bytes accessed | tf_op | source)
XLA Modules:
  0.0 71.6 jit_solution(15513439018038054369)
XLA Ops:
  0.6 65.8 %step_kernel.1 = (bf16[2,2,4,4,112,128]{5,4,3,2,1,0:T(8,128)(2,1)}, bf16[512,256]{1,0:T(8,128)(2,1)}, f32[8,256]{1,0:T(8,128)}) custom-call(bf16[256,3584]{1,0:T(8,128)(2,1)} %g_hbm.3, bf16[256,3584]{1,0:T(8,128)(2,1)} %m_hbm.3, bf16[3584,256]{1,0:T(8,128)(2,1)} %b_hbm.1), custom_call_target="tpu_custom_call" | custom-call | tf_op jit(solution)/shard_map/step_kernel/pallas_call | solution.py:426
  66.4 5.1 %output_kernel.1 = (bf16[256,3584]{1,0:T(8,128)(2,1)}, bf16[256,3584]{1,0:T(8,128)(2,1)}, bf16[3584,256]{1,0:T(8,128)(2,1)}) custom-call(bf16[256,3584]{1,0:T(8,128)(2,1)} %g_hbm.3, bf16[256,3584]{1,0:T(8,128)(2,1)} %m_hbm.3, bf16[512,256]{1,0:T(8,128)(2,1)} %get-tuple-element.6.both_hbm, bf16[2,3584,128]{2,1,0:T(8,128)(2,1)} %bitcast.1, ...), custom_call_target="tpu_custom_call" | custom-call | tf_op jit(solution)/shard_map/output_kernel/pallas_call | solution.py:454

commit v7 on v6

--- a/solution.py
+++ b/solution.py
@@ -34,6 +34,10 @@
 
 def lane_of(tile, j):
     return jnp.broadcast_to(tile[j:j + 1, :], tile.shape)
+
+
+def column_of(tile, j):
+    return jnp.broadcast_to(tile[:, j:j + 1], tile.shape)
 
 
 def reciprocal(v):
@@ -58,13 +62,14 @@
         for a in range(tiles):
             M_[a].append(jnp.where(ln + home * 128 == rows + (r0 + 8 * a), 1.0, 0.0))
         piv = [jnp.ones((8, 128), F32) for _ in range(tiles)]
-        for s in range(b // s8):
+        ahead = None
+        for s in range(tiles):
+            lane = r0 - home * 128 + s * s8
             C = []
             for k in range(s8):
-                lane = r0 - home * 128 + s * s8 + k
-                C.append([
-                    jnp.broadcast_to(M_[a][home][:, lane:lane + 1], (8, 128)) if a >= s else None for a in range(tiles)
-                ])
+                C.append([column_of(M_[a][home], lane + k) if a > s else None for a in range(tiles)])
+                C[k][s] = column_of(M_[s][home], lane + k) if ahead is None else ahead[k]
+            ahead = [column_of(M_[s + 1][home], lane + s8 + k) for k in range(s8)] if s + 1 < tiles else None
             for j in range(0, s8, 2):
                 first, second = C[j], C[j + 1]
                 p11 = lane_of(first[s], j)
@@ -75,10 +80,15 @@
                 mult = p12 * inv1
                 inv2 = p11 * reciprocal(det)
                 w1 = [first[a] * inv1 if a >= s else None for a in range(tiles)]
-                w2 = [(second[a] - first[a] * mult) * inv2 if a >= s else None for a in range(tiles)]
+                second = [second[a] - first[a] * mult if a >= s else None for a in range(tiles)]
+                w2 = [second[a] * inv2 if a >= s else None for a in range(tiles)]
+                if ahead is not None:
+                    for k in range(s8):
+                        b1, b2 = lane_of(first[s + 1], k), lane_of(second[s + 1], k)
+                        ahead[k] = (ahead[k] - w1[s + 1] * b1) - w2[s + 1] * b2
                 for k in range(j + 2, s8):
                     b1 = lane_of(first[s], k)
-                    b2 = lane_of(second[s], k) - b1 * mult
+                    b2 = lane_of(second[s], k)
                     for a in range(s, tiles):
                         C[k][a] = (C[k][a] - w1[a] * b1) - w2[a] * b2
                 w1[s] = jnp.where(rows > j, w1[s], 0.0)
@@ -144,6 +154,9 @@
     def dev(self, px, py, pc):
         return ((py * NX + px) * 2 + pc, self.t)
 
+    def y_x(self, i, j):
+        return self.ys[j] * NX + self.xs[i]
+
     def greet(self, devices):
         barrier = pltpu.get_barrier_semaphore()
         for device in devices:
@@ -173,7 +186,7 @@
 
 
 def step_kernel(g_hbm, m_hbm, b_hbm, result, both, inverse, gbuf, mbuf, bbuf, bht, part, rz, left, gpart, rg, own, r2, gram,
-                out, rs, r, rc, r16, f1, sab, s16, f2, sq, qc, qp, qz, load, store, ssem, rsem):
+                out, rs, r, rc, r16, f1, sab, s16, f2, sq, qc, qp, qz, load, store, gsem, hsem, zsem, ssem, rsem):
     at = Place(ssem, rsem)
     core, other, x, y, xs, ys = at.core, at.other, at.x, at.y, at.xs, at.ys
     nc = COLS // STEP
@@ -213,15 +226,55 @@
     left[piece(at.t, zr), :] = mine
     az = [at.share(left.at[piece(at.t, zr), :], at.zdev[j]) for j in range(1, NZ)]
 
-    gr = RANK // NF
-    gpart[...] = dot(mine, mine, 0, 0)
-    cps = [at.exchange(gpart.at[piece(at.all[j], gr), :], rg.at[j - 1], at.fdev[j]) for j in range(1, NF)]
-    acc = gpart[piece(at.f, gr), :]
-    for j in range(1, NF):
-        cps[j - 1].wait_recv()
-        acc = acc + rg[j - 1]
-    own[...] = acc
-    cps = [at.exchange(own, r2.at[j - 1], at.zdev[j]) for j in range(1, NZ)]
+    full = dot(mine, mine, 0, 0)
+    gpart[:, 0:8, :] = full[:128, :128].reshape(16, 8, 128)
+    gpart[:, 8:16, :] = full[:128, 128:].reshape(16, 8, 128)
+    gpart[:, 16:24, :] = full[128:, 128:].reshape(16, 8, 128)
+    owner = lax.rem(x + y, 2) == core
+    chips = [(i, j) for i in range(NX) for j in range(NY)]
+
+    def to_owner(k, slot):
+        i, j = chips[k]
+        device = at.dev(xs[i], ys[j], lax.rem(xs[i] + ys[j], 2))
+        return pltpu.make_async_remote_copy(
+            src_ref=gpart.at[at.y_x(i, j)], dst_ref=rg.at[slot], send_sem=gsem.at[k], recv_sem=gsem.at[16 + slot],
+            device_id=device if k else at.sibling, device_id_type=MESH,
+        )
+
+    scattered = [to_owner(k, 2 * k - 1 + core if k else 0) for k in range(16)]
+
+    @pl.when(jnp.logical_not(owner))
+    def _():
+        scattered[0].start()
+
+    for k in range(1, 16):
+        scattered[k].start()
+
+    def to_all(k, c):
+        i, j = chips[k]
+        return pltpu.make_async_remote_copy(
+            src_ref=gram.at[at.chip], dst_ref=gram.at[at.chip], send_sem=hsem.at[2 * k + c], recv_sem=hsem.at[32 + k],
+            device_id=at.dev(xs[i], ys[j], c) if k else at.sibling, device_id_type=MESH,
+        )
+
+    gathered = [to_all(0, 0)] + [to_all(k, c) for k in range(1, 16) for c in range(2)]
+    across = [
+        pltpu.make_async_remote_copy(
+            src_ref=own, dst_ref=r2.at[j - 1], send_sem=zsem.at[j], recv_sem=zsem.at[8 + j],
+            device_id=at.zdev[j], device_id_type=MESH,
+        )
+        for j in range(1, NZ)
+    ]
+
+    @pl.when(owner)
+    def _():
+        acc = gpart[at.chip]
+        for slot in range(31):
+            to_owner(0, slot).wait_recv()
+            acc = acc + rg[slot]
+        own[...] = acc
+        for cp in across:
+            cp.start()
 
     for cp in az:
         cp.wait_recv()
@@ -240,12 +293,17 @@
         product(k, other, rs)
         qs = pl.ds(k * qk, qk)
         cc.append([at.exchange(rs.at[h, qs], rc.at[h, qs], at.sibling) for h in range(2)])
-    for j in range(1, NZ):
-        cps[j - 1].wait_recv()
-        acc = acc + r2[j - 1]
-    grow = piece(at.f, gr)
-    gram[grow, :] = acc
-    ga = [at.share(gram.at[grow, :], at.fdev[j]) for j in range(1, NF)]
+
+    @pl.when(owner)
+    def _():
+        acc = own[...]
+        for j in range(1, NZ):
+            across[j - 1].wait_recv()
+            acc = acc + r2[j - 1]
+        gram[at.chip] = acc
+        for cp in gathered:
+            cp.start()
+
     for k in range(nk):
         product(k, core, r)
     for k in range(nk):
@@ -259,8 +317,16 @@
     for j in range(1, NX):
         one[0].append(at.exchange(r16.at[0, xs[j]], f1.at[0, j - 1], at.dev(xs[j], y, core)))
         one[1].append(at.exchange(r16.at[1, :, ys[j]], f1.at[1, j - 1], at.dev(x, ys[j], core)))
-    for cp in ga:
-        cp.wait_recv()
+    for k in range(1, 16):
+        to_all(k, 0).wait_recv()
+
+    @pl.when(jnp.logical_not(owner))
+    def _():
+        to_all(0, 0).wait_recv()
+
+    upper = jnp.concatenate([gram[:, 0:8, :].reshape(128, 128), gram[:, 8:16, :].reshape(128, 128)], axis=1)
+    corner = gram[:, 16:24, :].reshape(128, 128)
+    full = jnp.concatenate([upper, jnp.concatenate([jnp.zeros_like(corner), corner], axis=1)], axis=0)
     two = [[], []]
 
     def second_stage():
@@ -277,7 +343,7 @@
                 else:
                     two[h].append(at.exchange(s16.at[h, xs[j]], f2.at[h, j - 1], at.dev(xs[j], y, core)))
 
-    w = lower_inverse(gram[...], {2: second_stage})
+    w = lower_inverse(full, {2: second_stage})
     ortho = dot(left[...].astype(F32), w, 1, 1, HI)
     both[0:ROWS, :] = ortho.astype(BF16)
     halves = []
@@ -368,6 +434,18 @@
         cp.wait_recv()
         keep(h, q, k, other)
     at.finish()
+    for k in range(1, 16):
+        scattered[k].wait_send()
+
+    @pl.when(jnp.logical_not(owner))
+    def _():
+        scattered[0].wait_send()
+
+    @pl.when(owner)
+    def _():
+        for cp in across + gathered:
+            cp.wait_send()
+
     for cp in stores:
         cp.wait()
 
@@ -421,8 +499,7 @@
 def body(grad, momentum, basis):
     dma = pltpu.SemaphoreType.DMA
     zr = ROWS // NZ
-    gr = RANK // NF
-    sends = 7 + 7 + 31 + 7 + 31 + 4 + 6 + 6 + 6 + 1 + 15 + 8 + 2 + 7 + 4 + 8
+    sends = 7 + 7 + 4 + 6 + 6 + 6 + 1 + 15 + 8 + 2 + 7 + 4 + 8
     right, both, inverse = pl.pallas_call(
         step_kernel,
         out_shape=(
@@ -436,15 +513,15 @@
             pltpu.VMEM((ROWS, COLS), BF16), pltpu.VMEM((ROWS, COLS), BF16), pltpu.VMEM((COLS, RANK), BF16),
             pltpu.VMEM((COLS, RANK), BF16),
             pltpu.VMEM((ROWS, RANK), BF16), pltpu.VMEM((NZ - 1, zr, RANK), BF16), pltpu.VMEM((ROWS, RANK), BF16),
-            pltpu.VMEM((RANK, RANK), F32), pltpu.VMEM((NF - 1, gr, RANK), F32),
-            pltpu.VMEM((gr, RANK), F32), pltpu.VMEM((NZ - 1, gr, RANK), F32), pltpu.VMEM((RANK, RANK), F32),
+            pltpu.VMEM((16, 24, 128), F32), pltpu.VMEM((31, 24, 128), F32),
+            pltpu.VMEM((24, 128), F32), pltpu.VMEM((NZ - 1, 24, 128), F32), pltpu.VMEM((16, 24, 128), F32),
             pltpu.VMEM((2, 2, NX, NY, BLOCK, 128), BF16), pltpu.VMEM((2, NX, NY, BLOCK, 128), BF16),
             pltpu.VMEM((2, NX, NY, BLOCK, 128), F32), pltpu.VMEM((2, NX, NY, BLOCK, 128), BF16),
             pltpu.VMEM((2, NX, NY, BLOCK, 128), BF16), pltpu.VMEM((2, 3, 4, BLOCK, 128), BF16),
             pltpu.VMEM((2, 4, BLOCK, 128), F32), pltpu.VMEM((2, 4, BLOCK, 128), BF16), pltpu.VMEM((2, 3, BLOCK, 128), BF16),
             pltpu.VMEM((8, 128), F32), pltpu.VMEM((8, 128), F32),
             pltpu.VMEM((NX * NY, 8, 128), F32), pltpu.VMEM((NZ, 8, 128), F32),
-            dma((3 * (COLS // STEP),)), dma((20,)), dma((sends,)), dma((sends,)),
+            dma((3 * (COLS // STEP),)), dma((20,)), dma((47,)), dma((48,)), dma((16,)), dma((sends,)), dma((sends,)),
         ],
         compiler_params=pltpu.CompilerParams(collective_id=0, has_side_effects=True, vmem_limit_bytes=VMEM_LIMIT),
         name="step_kernel",

time: 71.6 us -> 68.5 us (0.957)
  Pallas kernels: 70.9 us -> 67.6 us
    pallas_call x1, Pallas kernels: 65.8 us -> 62.5 us  [body(): pl.pallas_call(step_kernel, out_shape=(jax.ShapeDtypeStruct((2, 2, NX, NY...]
where the time goes in v7:
time: 68.5 us; the launch traced here: 68.4 us
  Pallas kernels  67.6 us (99%)
  between operations  0.8 us (1%)
    pallas_call x1, Pallas kernels, body(): pl.pallas_call(step_kernel, out_shape=(jax.ShapeDtypeStruct((2, 2, NX, NY...  62.5 us
    pallas_call x1, Pallas kernels, body(): pl.pallas_call(output_kernel, out_shape=(jax.ShapeDtypeStruct((ROWS, COLS...  5.11 us

profile of v7, /device:TPU:1, one launch (start us, length us, event | category | flops | bytes accessed | tf_op | source)
XLA Modules:
  0.0 68.4 jit_solution(9003828660964490302)
XLA Ops:
  0.6 62.5 %step_kernel.1 = (bf16[2,2,4,4,112,128]{5,4,3,2,1,0:T(8,128)(2,1)}, bf16[512,256]{1,0:T(8,128)(2,1)}, f32[8,256]{1,0:T(8,128)}) custom-call(bf16[256,3584]{1,0:T(8,128)(2,1)} %g_hbm.3, bf16[256,3584]{1,0:T(8,128)(2,1)} %m_hbm.3, bf16[3584,256]{1,0:T(8,128)(2,1)} %b_hbm.1), custom_call_target="tpu_custom_call" | custom-call | tf_op jit(solution)/shard_map/step_kernel/pallas_call | solution.py:503
  63.1 5.1 %output_kernel.1 = (bf16[256,3584]{1,0:T(8,128)(2,1)}, bf16[256,3584]{1,0:T(8,128)(2,1)}, bf16[3584,256]{1,0:T(8,128)(2,1)}) custom-call(bf16[256,3584]{1,0:T(8,128)(2,1)} %g_hbm.3, bf16[256,3584]{1,0:T(8,128)(2,1)} %m_hbm.3, bf16[512,256]{1,0:T(8,128)(2,1)} %get-tuple-element.6.both_hbm, bf16[2,3584,128]{2,1,0:T(8,128)(2,1)} %bitcast.1, ...), custom_call_target="tpu_custom_call" | custom-call | tf_op jit(solution)/shard_map/output_kernel/pallas_call | solution.py:531

commit v8 on v7

--- a/solution.py
+++ b/solution.py
@@ -151,6 +151,11 @@
             (self.ys, self.dev(self.x, self.ys[1], self.core), self.dev(self.x, self.ys[3], self.core)),
         )
 
+        self.twins = (
+            (self.dev(self.xs[1], self.y, self.other), self.dev(self.xs[3], self.y, self.other)),
+            (self.dev(self.x, self.ys[1], self.other), self.dev(self.x, self.ys[3], self.other)),
+        )
+
     def dev(self, px, py, pc):
         return ((py * NX + px) * 2 + pc, self.t)
 
@@ -186,7 +191,7 @@
 
 
 def step_kernel(g_hbm, m_hbm, b_hbm, result, both, inverse, gbuf, mbuf, bbuf, bht, part, rz, left, gpart, rg, own, r2, gram,
-                out, rs, r, rc, r16, f1, sab, s16, f2, sq, qc, qp, qz, load, store, gsem, hsem, zsem, ssem, rsem):
+                out, rs, r, rc, r16, f1, joined, sab, s16, f2, sq, qc, qp, qz, load, store, gsem, hsem, zsem, ssem, rsem):
     at = Place(ssem, rsem)
     core, other, x, y, xs, ys = at.core, at.other, at.x, at.y, at.xs, at.ys
     nc = COLS // STEP
@@ -313,10 +318,27 @@
             total = r[h, qs] + rc[h, qs].astype(F32)
             r[h, qs] = total
             r16[h, qs] = total.astype(BF16)
-    one = [[], []]
-    for j in range(1, NX):
-        one[0].append(at.exchange(r16.at[0, xs[j]], f1.at[0, j - 1], at.dev(xs[j], y, core)))
-        one[1].append(at.exchange(r16.at[1, :, ys[j]], f1.at[1, j - 1], at.dev(x, ys[j], core)))
+
+    def half_of(ref, h, q, k):
+        return ref.at[0, q, pl.ds(2 * k, 2)] if h == 0 else ref.at[1, pl.ds(2 * k, 2), q]
+
+    one = []
+    for h in range(2):
+        pos, nxt, prv = at.ways[h]
+        one.append([
+            at.exchange(half_of(r16, h, pos[2], 0), f1.at[h, 0], nxt), at.exchange(half_of(r16, h, pos[2], 1), f1.at[h, 1], prv),
+        ])
+    for h in range(2):
+        pos, nxt, prv = at.ways[h]
+        one[h] += [
+            at.exchange(half_of(r16, h, pos[1], 1), f1.at[h, 2], nxt), at.exchange(half_of(r16, h, pos[3], 0), f1.at[h, 3], prv),
+        ]
+    for h in range(2):
+        pos, nxt, prv = at.ways[h]
+        for k, (q, to) in enumerate(((pos[1], nxt), (pos[3], prv))):
+            one[h][k].wait_recv()
+            joined[h, k] = (half_of(r, h, q, k)[...] + f1[h, k].astype(F32)).astype(BF16)
+            one[h].append(at.exchange(joined.at[h, k], f1.at[h, 4 + k], to))
     for k in range(1, 16):
         to_all(k, 0).wait_recv()
 
@@ -331,12 +353,12 @@
 
     def second_stage():
         for h in range(2):
-            total = r[0, x] if h == 0 else r[1, :, y]
-            for j in range(1, NX):
-                one[h][j - 1].wait_recv()
-                total = total + f1[h, j - 1].astype(F32)
-            sab[h] = total
-            s16[h] = total.astype(BF16)
+            for k in range(2, 6):
+                one[h][k].wait_recv()
+            for k in range(2):
+                total = half_of(r, h, x if h == 0 else y, k)[...] + f1[h, 3 - k].astype(F32) + f1[h, 4 + k].astype(F32)
+                sab[h, 2 * k:2 * k + 2] = total
+                s16[h, 2 * k:2 * k + 2] = total.astype(BF16)
             for j in range(1, NX):
                 if h == 0:
                     two[h].append(at.exchange(s16.at[h, ys[j]], f2.at[h, j - 1], at.dev(x, ys[j], core)))
@@ -407,10 +429,9 @@
     relays = []
     for h in range(2):
         pos, nxt, prv = at.ways[h]
-        begun[h][0].wait_recv()
-        relays.append(at.share(band(h, pos[3], 0), nxt))
-        begun[h][1].wait_recv()
-        relays.append(at.share(band(h, pos[1], 1), prv))
+        for k, (q, near, far) in enumerate(((pos[3], nxt, at.twins[h][0]), (pos[1], prv, at.twins[h][1]))):
+            begun[h][k].wait_recv()
+            relays.append((at.share(band(h, q, k), near), at.share(band(h, q, k), far)))
     for cp in sz:
         cp.wait_recv()
     total = qz[0]
@@ -425,14 +446,17 @@
         forward(h, pos[3])
         begun[h][3].wait_recv()
         forward(h, pos[1])
-    for h in range(2):
-        pos = at.ways[h][0]
-        for k in range(2):
-            relays[2 * h + k].wait_recv()
-            forward(h, pos[2], k)
     for cp, (h, q, k) in zip(last, spans):
         cp.wait_recv()
         keep(h, q, k, other)
+    for h in range(2):
+        pos = at.ways[h][0]
+        for k in range(2):
+            near, far = relays[2 * h + k]
+            near.wait_recv()
+            keep(h, pos[2], k, core)
+            far.wait_recv()
+            keep(h, pos[2], k, other)
     at.finish()
     for k in range(1, 16):
         scattered[k].wait_send()
@@ -499,7 +523,7 @@
 def body(grad, momentum, basis):
     dma = pltpu.SemaphoreType.DMA
     zr = ROWS // NZ
-    sends = 7 + 7 + 4 + 6 + 6 + 6 + 1 + 15 + 8 + 2 + 7 + 4 + 8
+    sends = 7 + 7 + 4 + 12 + 6 + 6 + 1 + 15 + 8 + 6 + 7 + 8
     right, both, inverse = pl.pallas_call(
         step_kernel,
         out_shape=(
@@ -517,7 +541,7 @@
             pltpu.VMEM((24, 128), F32), pltpu.VMEM((NZ - 1, 24, 128), F32), pltpu.VMEM((16, 24, 128), F32),
             pltpu.VMEM((2, 2, NX, NY, BLOCK, 128), BF16), pltpu.VMEM((2, NX, NY, BLOCK, 128), BF16),
             pltpu.VMEM((2, NX, NY, BLOCK, 128), F32), pltpu.VMEM((2, NX, NY, BLOCK, 128), BF16),
-            pltpu.VMEM((2, NX, NY, BLOCK, 128), BF16), pltpu.VMEM((2, 3, 4, BLOCK, 128), BF16),
+            pltpu.VMEM((2, NX, NY, BLOCK, 128), BF16), pltpu.VMEM((2, 6, 2, BLOCK, 128), BF16), pltpu.VMEM((2, 2, 2, BLOCK, 128), BF16),
             pltpu.VMEM((2, 4, BLOCK, 128), F32), pltpu.VMEM((2, 4, BLOCK, 128), BF16), pltpu.VMEM((2, 3, BLOCK, 128), BF16),
             pltpu.VMEM((8, 128), F32), pltpu.VMEM((8, 128), F32),
             pltpu.VMEM((NX * NY, 8, 128), F32), pltpu.VMEM((NZ, 8, 128), F32),

time: 68.5 us -> 68.6 us (level)
  no operation moved by 1% of the time
where the time goes in v8:
time: 68.6 us; the launch traced here: 68.5 us
  Pallas kernels  67.7 us (99%)
  between operations  0.8 us (1%)
    pallas_call x1, Pallas kernels, body(): pl.pallas_call(step_kernel, out_shape=(jax.ShapeDtypeStruct((2, 2, NX, NY...  62.6 us
    pallas_call x1, Pallas kernels, body(): pl.pallas_call(output_kernel, out_shape=(jax.ShapeDtypeStruct((ROWS, COLS...  5.11 us

profile of v8, /device:TPU:1, one launch (start us, length us, event | category | flops | bytes accessed | tf_op | source)
XLA Modules:
  0.0 68.5 jit_solution(15129769345214040402)
XLA Ops:
  0.6 62.6 %step_kernel.1 = (bf16[2,2,4,4,112,128]{5,4,3,2,1,0:T(8,128)(2,1)}, bf16[512,256]{1,0:T(8,128)(2,1)}, f32[8,256]{1,0:T(8,128)}) custom-call(bf16[256,3584]{1,0:T(8,128)(2,1)} %g_hbm.3, bf16[256,3584]{1,0:T(8,128)(2,1)} %m_hbm.3, bf16[3584,256]{1,0:T(8,128)(2,1)} %b_hbm.1), custom_call_target="tpu_custom_call" | custom-call | tf_op jit(solution)/shard_map/step_kernel/pallas_call | solution.py:527
  63.2 5.1 %output_kernel.1 = (bf16[256,3584]{1,0:T(8,128)(2,1)}, bf16[256,3584]{1,0:T(8,128)(2,1)}, bf16[3584,256]{1,0:T(8,128)(2,1)}) custom-call(bf16[256,3584]{1,0:T(8,128)(2,1)} %g_hbm.3, bf16[256,3584]{1,0:T(8,128)(2,1)} %m_hbm.3, bf16[512,256]{1,0:T(8,128)(2,1)} %get-tuple-element.6.both_hbm, bf16[2,3584,128]{2,1,0:T(8,128)(2,1)} %bitcast.1, ...), custom_call_target="tpu_custom_call" | custom-call | tf_op jit(solution)/shard_map/output_kernel/pallas_call | solution.py:555

commit v9 on v8

--- a/solution.py
+++ b/solution.py
@@ -181,10 +181,6 @@
     def share(self, ref, device):
         return self.exchange(ref, ref, device)
 
-    def finish(self):
-        for cp in self.sends:
-            cp.wait_send()
-
 
 def piece(z, size):
     return pl.ds(pl.multiple_of(z * size, size), size)
@@ -366,8 +362,6 @@
                     two[h].append(at.exchange(s16.at[h, xs[j]], f2.at[h, j - 1], at.dev(xs[j], y, core)))
 
     w = lower_inverse(full, {2: second_stage})
-    ortho = dot(left[...].astype(F32), w, 1, 1, HI)
-    both[0:ROWS, :] = ortho.astype(BF16)
     halves = []
     for h in range(2):
         total = sab[h, y if h == 0 else x]
@@ -379,20 +373,19 @@
     rounded = right.astype(BF16)
     for h in range(2):
         out[h, core, x, y] = rounded[:, 128 * h:128 * h + 128]
-    g2 = []
-    for j in range(1, NX):
-        g2.append(at.share(out.at[0, core, x, y], at.dev(x, ys[j], core)))
-        g2.append(at.share(out.at[1, core, x, y], at.dev(xs[j], y, core)))
+    g2 = [[], []]
+    for j in (2, 1, 3):
+        g2[0].append(at.share(out.at[0, core, x, y], at.dev(x, ys[j], core)))
+        g2[1].append(at.share(out.at[1, core, x, y], at.dev(xs[j], y, core)))
     total = jnp.sum(right * right, axis=0, keepdims=True)
     srow = lax.broadcasted_iota(jnp.int32, (8, 128), 0)
     sq[...] = jnp.where(srow == 0, total[:, :128], total[:, 128:])
     sc = at.exchange(sq, qc, at.sibling)
+    ortho = dot(left[...].astype(F32), w, 1, 1, HI)
+    both[0:ROWS, :] = ortho.astype(BF16)
     sc.wait_recv()
     qp[at.chip] = sq[...] + qc[...]
     sp = [at.share(qp.at[at.chip], device) for device in at.plane]
-    for cp in g2:
-        cp.wait_recv()
-
     def band(h, q, k=None, ref=out, pc=core):
         if k is None:
             return ref.at[0, pc, q] if h == 0 else ref.at[1, pc, :, q]
@@ -412,13 +405,16 @@
 
     begun = []
     for h in range(2):
+        for cp in g2[h]:
+            cp.wait_recv()
         pos, nxt, prv = at.ways[h]
-        begun.append([at.share(band(h, pos[0], 0), nxt), at.share(band(h, pos[0], 1), prv)])
-    for h in range(2):
-        pos, nxt, prv = at.ways[h]
-        begun[h] += [at.share(band(h, pos[0], 1), nxt), at.share(band(h, pos[0], 0), prv)]
+        begun.append([
+            at.share(band(h, pos[0], 0), nxt), at.share(band(h, pos[0], 1), prv),
+            at.share(band(h, pos[0], 1), nxt), at.share(band(h, pos[0], 0), prv),
+        ])
     for h in range(2):
         forward(h, at.ways[h][0][0])
+    old = len(at.sends) - 10
     for cp in sp:
         cp.wait_recv()
     total = qp[0]
@@ -432,6 +428,24 @@
         for k, (q, near, far) in enumerate(((pos[3], nxt, at.twins[h][0]), (pos[1], prv, at.twins[h][1]))):
             begun[h][k].wait_recv()
             relays.append((at.share(band(h, q, k), near), at.share(band(h, q, k), far)))
+    for h in range(2):
+        pos = at.ways[h][0]
+        begun[h][2].wait_recv()
+        forward(h, pos[3])
+        begun[h][3].wait_recv()
+        forward(h, pos[1])
+    for cp in at.sends[:old] + scattered[1:]:
+        cp.wait_send()
+
+    @pl.when(jnp.logical_not(owner))
+    def _():
+        scattered[0].wait_send()
+
+    @pl.when(owner)
+    def _():
+        for cp in across + gathered:
+            cp.wait_send()
+
     for cp in sz:
         cp.wait_recv()
     total = qz[0]
@@ -440,12 +454,6 @@
     scale = jnp.sqrt(jnp.concatenate([total[0:1, :], total[1:2, :]], axis=1) / N + 1e-06)
     inverse[...] = jnp.broadcast_to(1.0 / scale, (8, RANK))
     both[ROWS:, :] = (ortho * (math.sqrt(M / RANK) / scale)).astype(BF16)
-    for h in range(2):
-        pos = at.ways[h][0]
-        begun[h][2].wait_recv()
-        forward(h, pos[3])
-        begun[h][3].wait_recv()
-        forward(h, pos[1])
     for cp, (h, q, k) in zip(last, spans):
         cp.wait_recv()
         keep(h, q, k, other)
@@ -457,19 +465,8 @@
             keep(h, pos[2], k, core)
             far.wait_recv()
             keep(h, pos[2], k, other)
-    at.finish()
-    for k in range(1, 16):
-        scattered[k].wait_send()
-
-    @pl.when(jnp.logical_not(owner))
-    def _():
-        scattered[0].wait_send()
-
-    @pl.when(owner)
-    def _():
-        for cp in across + gathered:
-            cp.wait_send()
-
+    for cp in at.sends[old:]:
+        cp.wait_send()
     for cp in stores:
         cp.wait()
 

time: 68.6 us -> 67.5 us (0.984)
  Pallas kernels: 67.7 us -> 66.6 us
    pallas_call x1, Pallas kernels: 62.6 us -> 61.5 us  [body(): pl.pallas_call(step_kernel, out_shape=(jax.ShapeDtypeStruct((2, 2, NX, NY...]
where the time goes in v9:
time: 67.5 us; the launch traced here: 67.4 us
  Pallas kernels  66.6 us (99%)
  between operations  0.8 us (1%)
    pallas_call x1, Pallas kernels, body(): pl.pallas_call(step_kernel, out_shape=(jax.ShapeDtypeStruct((2, 2, NX, NY...  61.5 us
    pallas_call x1, Pallas kernels, body(): pl.pallas_call(output_kernel, out_shape=(jax.ShapeDtypeStruct((ROWS, COLS...  5.11 us

profile of v9, /device:TPU:1, one launch (start us, length us, event | category | flops | bytes accessed | tf_op | source)
XLA Modules:
  0.0 67.4 jit_solution(16936417316642980645)
XLA Ops:
  0.6 61.5 %step_kernel.1 = (bf16[2,2,4,4,112,128]{5,4,3,2,1,0:T(8,128)(2,1)}, bf16[512,256]{1,0:T(8,128)(2,1)}, f32[8,256]{1,0:T(8,128)}) custom-call(bf16[256,3584]{1,0:T(8,128)(2,1)} %g_hbm.3, bf16[256,3584]{1,0:T(8,128)(2,1)} %m_hbm.3, bf16[3584,256]{1,0:T(8,128)(2,1)} %b_hbm.1), custom_call_target="tpu_custom_call" | custom-call | tf_op jit(solution)/shard_map/step_kernel/pallas_call | solution.py:524
  62.1 5.1 %output_kernel.1 = (bf16[256,3584]{1,0:T(8,128)(2,1)}, bf16[256,3584]{1,0:T(8,128)(2,1)}, bf16[3584,256]{1,0:T(8,128)(2,1)}) custom-call(bf16[256,3584]{1,0:T(8,128)(2,1)} %g_hbm.3, bf16[256,3584]{1,0:T(8,128)(2,1)} %m_hbm.3, bf16[512,256]{1,0:T(8,128)(2,1)} %get-tuple-element.6.both_hbm, bf16[2,3584,128]{2,1,0:T(8,128)(2,1)} %bitcast.1, ...), custom_call_target="tpu_custom_call" | custom-call | tf_op jit(solution)/shard_map/output_kernel/pallas_call | solution.py:552

commit v10 on v9

--- a/solution.py
+++ b/solution.py
@@ -43,6 +43,11 @@
 def reciprocal(v):
     near = pl.reciprocal(v, approx=True)
     return near * (2.0 - v * near)
+
+
+def parts(v):
+    hi = v.astype(BF16)
+    return hi, (v - hi.astype(F32)).astype(BF16)
 
 
 def lower_inverse(gram, beside, b=64, s8=8):
@@ -112,10 +117,12 @@
         if p + 1 < n // b:
             r1 = r0 + b
             cut = r1 // 128 * 128
-            upd = dot(U[:, cut:], U, 0, 0, HI)
+            hi, lo = parts(U)
+            lhs = jnp.concatenate([hi[:, cut:], hi[:, cut:], lo[:, cut:], lo[:, cut:]], axis=0).T
+            rhs = jnp.concatenate([hi, lo, hi, lo], axis=0)
             for q in range(p + 1, n // b):
                 old = jnp.where((lanes >= r0) & (lanes < r1), 0.0, panels[q])
-                panels[q] = old - upd[q * b - cut:(q + 1) * b - cut, :]
+                panels[q] = old - dot(lhs[q * b - cut:(q + 1) * b - cut, :], rhs, 1, 0)
             if p in beside:
                 beside[p]()
     W = jnp.concatenate(done, axis=0)
@@ -307,19 +314,17 @@
 
     for k in range(nk):
         product(k, core, r)
-    for k in range(nk):
-        qs = pl.ds(k * qk, qk)
-        for h in range(2):
+    def half_of(ref, h, q, k):
+        return ref.at[0, q, pl.ds(2 * k, 2)] if h == 0 else ref.at[1, pl.ds(2 * k, 2), q]
+
+    one = []
+    for h in range(2):
+        for k in range(nk):
+            qs = pl.ds(k * qk, qk)
             cc[k][h].wait_recv()
             total = r[h, qs] + rc[h, qs].astype(F32)
             r[h, qs] = total
             r16[h, qs] = total.astype(BF16)
-
-    def half_of(ref, h, q, k):
-        return ref.at[0, q, pl.ds(2 * k, 2)] if h == 0 else ref.at[1, pl.ds(2 * k, 2), q]
-
-    one = []
-    for h in range(2):
         pos, nxt, prv = at.ways[h]
         one.append([
             at.exchange(half_of(r16, h, pos[2], 0), f1.at[h, 0], nxt), at.exchange(half_of(r16, h, pos[2], 1), f1.at[h, 1], prv),
@@ -362,6 +367,7 @@
                     two[h].append(at.exchange(s16.at[h, xs[j]], f2.at[h, j - 1], at.dev(xs[j], y, core)))
 
     w = lower_inverse(full, {2: second_stage})
+    whi, wlo = parts(w)
     halves = []
     for h in range(2):
         total = sab[h, y if h == 0 else x]
@@ -369,7 +375,9 @@
             two[h][j - 1].wait_recv()
             total = total + f2[h, j - 1].astype(F32)
         halves.append(total)
-    right = dot(jnp.concatenate(halves, axis=1), w, 1, 1, HI)
+    hi, lo = parts(jnp.concatenate(halves, axis=1))
+    right = dot(jnp.concatenate([hi, lo], axis=0), whi, 1, 1)
+    right = right[:BLOCK] + right[BLOCK:] + dot(hi, wlo, 1, 1)
     rounded = right.astype(BF16)
     for h in range(2):
         out[h, core, x, y] = rounded[:, 128 * h:128 * h + 128]
@@ -381,7 +389,7 @@
     srow = lax.broadcasted_iota(jnp.int32, (8, 128), 0)
     sq[...] = jnp.where(srow == 0, total[:, :128], total[:, 128:])
     sc = at.exchange(sq, qc, at.sibling)
-    ortho = dot(left[...].astype(F32), w, 1, 1, HI)
+    ortho = dot(left[...], whi, 1, 1) + dot(left[...], wlo, 1, 1)
     both[0:ROWS, :] = ortho.astype(BF16)
     sc.wait_recv()
     qp[at.chip] = sq[...] + qc[...]
@@ -474,29 +482,33 @@
 def output_kernel(g_hbm, m_hbm, both_hbm, right_hbm, inv_hbm, update, new_momentum, new_basis,
                   gbuf, mbuf, both, rbuf, inv, ubuf, nbuf, bbuf, load, store):
     nc = COLS // STEP
-    first = [
-        pltpu.make_async_copy(both_hbm, both, load.at[4 * nc]),
-        pltpu.make_async_copy(inv_hbm, inv, load.at[4 * nc + 1]),
-    ]
     loads = []
-    for c in range(nc):
+
+    def fetch(c):
         cols = pl.ds(c * STEP, STEP)
         loads.append([
-            pltpu.make_async_copy(right_hbm.at[0, cols, :], rbuf.at[0, cols, :], load.at[4 * c]),
-            pltpu.make_async_copy(right_hbm.at[1, cols, :], rbuf.at[1, cols, :], load.at[4 * c + 1]),
-            pltpu.make_async_copy(g_hbm.at[:, cols], gbuf.at[:, cols], load.at[4 * c + 2]),
-            pltpu.make_async_copy(m_hbm.at[:, cols], mbuf.at[:, cols], load.at[4 * c + 3]),
+            pltpu.make_async_copy(right_hbm.at[:, cols, :], rbuf.at[:, cols, :], load.at[3 * c]),
+            pltpu.make_async_copy(g_hbm.at[:, cols], gbuf.at[:, cols], load.at[3 * c + 1]),
+            pltpu.make_async_copy(m_hbm.at[:, cols], mbuf.at[:, cols], load.at[3 * c + 2]),
         ])
+        for cp in loads[c]:
+            cp.start()
+
+    first = [
+        pltpu.make_async_copy(both_hbm, both, load.at[3 * nc]),
+        pltpu.make_async_copy(inv_hbm, inv, load.at[3 * nc + 1]),
+    ]
     for cp in first:
         cp.start()
-    for group in loads:
-        for cp in group:
-            cp.start()
+    for c in range(3):
+        fetch(c)
     for cp in first:
         cp.wait()
     stores = []
     for c in range(nc):
         cols = pl.ds(c * STEP, STEP)
+        if c + 3 < nc:
+            fetch(c + 3)
         for cp in loads[c]:
             cp.wait()
         rr = jnp.concatenate([rbuf[0, cols, :], rbuf[1, cols, :]], axis=1)
@@ -561,7 +573,7 @@
         scratch_shapes=[
             wide, wide, pltpu.VMEM((2 * ROWS, RANK), BF16), pltpu.VMEM((2, COLS, 128), BF16), pltpu.VMEM((8, RANK), F32),
             wide, wide, pltpu.VMEM((COLS, RANK), BF16),
-            dma((4 * nc + 2,)), dma((3 * nc,)),
+            dma((3 * nc + 2,)), dma((3 * nc,)),
         ],
         compiler_params=pltpu.CompilerParams(vmem_limit_bytes=VMEM_LIMIT),
         name="output_kernel",

time: 67.5 us -> 67.3 us (level)
    pallas_call x1, Pallas kernels: 61.5 us -> 60.5 us  [body(): pl.pallas_call(step_kernel, out_shape=(jax.ShapeDtypeStruct((2, 2, NX, NY...]
    pallas_call x1, Pallas kernels: 5.11 us -> 5.89 us  [body(): pl.pallas_call(output_kernel, out_shape=(jax.ShapeDtypeStruct((ROWS, COLS...]
where the time goes in v10:
time: 67.3 us; the launch traced here: 67.2 us
  Pallas kernels  66.4 us (99%)
  between operations  0.8 us (1%)
    pallas_call x1, Pallas kernels, body(): pl.pallas_call(step_kernel, out_shape=(jax.ShapeDtypeStruct((2, 2, NX, NY...  60.5 us
    pallas_call x1, Pallas kernels, body(): pl.pallas_call(output_kernel, out_shape=(jax.ShapeDtypeStruct((ROWS, COLS...  5.89 us

profile of v10, /device:TPU:1, one launch (start us, length us, event | category | flops | bytes accessed | tf_op | source)
XLA Modules:
  0.0 67.2 jit_solution(17282710902469999801)
XLA Ops:
  0.6 60.5 %step_kernel.1 = (bf16[2,2,4,4,112,128]{5,4,3,2,1,0:T(8,128)(2,1)}, bf16[512,256]{1,0:T(8,128)(2,1)}, f32[8,256]{1,0:T(8,128)}) custom-call(bf16[256,3584]{1,0:T(8,128)(2,1)} %g_hbm.3, bf16[256,3584]{1,0:T(8,128)(2,1)} %m_hbm.3, bf16[3584,256]{1,0:T(8,128)(2,1)} %b_hbm.1), custom_call_target="tpu_custom_call" | custom-call | tf_op jit(solution)/shard_map/step_kernel/pallas_call | solution.py:536
  61.1 5.9 %output_kernel.1 = (bf16[256,3584]{1,0:T(8,128)(2,1)}, bf16[256,3584]{1,0:T(8,128)(2,1)}, bf16[3584,256]{1,0:T(8,128)(2,1)}) custom-call(bf16[256,3584]{1,0:T(8,128)(2,1)} %g_hbm.3, bf16[256,3584]{1,0:T(8,128)(2,1)} %m_hbm.3, bf16[512,256]{1,0:T(8,128)(2,1)} %get-tuple-element.6.both_hbm, bf16[2,3584,128]{2,1,0:T(8,128)(2,1)} %bitcast.1, ...), custom_call_target="tpu_custom_call" | custom-call | tf_op jit(solution)/shard_map/output_kernel/pallas_call | solution.py:564

commit v11 on v10

--- a/solution.py
+++ b/solution.py
@@ -193,7 +193,7 @@
     return pl.ds(pl.multiple_of(z * size, size), size)
 
 
-def step_kernel(g_hbm, m_hbm, b_hbm, result, both, inverse, gbuf, mbuf, bbuf, bht, part, rz, left, gpart, rg, own, r2, gram,
+def step_kernel(g_hbm, m_hbm, b_hbm, result, both_hbm, inv_hbm, half_hbm, both, inverse, gbuf, mbuf, bbuf, bht, part, rz, left, gpart, rg, own, r2, gram,
                 out, rs, r, rc, r16, f1, joined, sab, s16, f2, sq, qc, qp, qz, load, store, gsem, hsem, zsem, ssem, rsem):
     at = Place(ssem, rsem)
     core, other, x, y, xs, ys = at.core, at.other, at.x, at.y, at.xs, at.ys
@@ -226,6 +226,8 @@
     for c in range(nc):
         cols = pl.ds(c * STEP, STEP)
         bht[cols, :] = gbuf[:, cols].T
+    kept = pltpu.make_async_copy(gbuf, half_hbm, store.at[20])
+    kept.start()
     mine = part[piece(at.t, zr), :].astype(F32)
     for j in range(1, NZ):
         cps[j - 1].wait_recv()
@@ -444,6 +446,7 @@
         forward(h, pos[1])
     for cp in at.sends[:old] + scattered[1:]:
         cp.wait_send()
+    kept.wait()
 
     @pl.when(jnp.logical_not(owner))
     def _():
@@ -462,6 +465,11 @@
     scale = jnp.sqrt(jnp.concatenate([total[0:1, :], total[1:2, :]], axis=1) / N + 1e-06)
     inverse[...] = jnp.broadcast_to(1.0 / scale, (8, RANK))
     both[ROWS:, :] = (ortho * (math.sqrt(M / RANK) / scale)).astype(BF16)
+    small = [
+        pltpu.make_async_copy(both, both_hbm, store.at[21]), pltpu.make_async_copy(inverse, inv_hbm, store.at[22]),
+    ]
+    for cp in small:
+        cp.start()
     for cp, (h, q, k) in zip(last, spans):
         cp.wait_recv()
         keep(h, q, k, other)
@@ -475,48 +483,42 @@
             keep(h, pos[2], k, other)
     for cp in at.sends[old:]:
         cp.wait_send()
-    for cp in stores:
+    for cp in stores + small:
         cp.wait()
 
 
-def output_kernel(g_hbm, m_hbm, both_hbm, right_hbm, inv_hbm, update, new_momentum, new_basis,
-                  gbuf, mbuf, both, rbuf, inv, ubuf, nbuf, bbuf, load, store):
+def output_kernel(half_hbm, both_hbm, right_hbm, inv_hbm, update, new_momentum, new_basis,
+                  hbuf, both, rbuf, inv, ubuf, nbuf, bbuf, load, store):
     nc = COLS // STEP
-    loads = []
-
-    def fetch(c):
-        cols = pl.ds(c * STEP, STEP)
-        loads.append([
-            pltpu.make_async_copy(right_hbm.at[:, cols, :], rbuf.at[:, cols, :], load.at[3 * c]),
-            pltpu.make_async_copy(g_hbm.at[:, cols], gbuf.at[:, cols], load.at[3 * c + 1]),
-            pltpu.make_async_copy(m_hbm.at[:, cols], mbuf.at[:, cols], load.at[3 * c + 2]),
-        ])
-        for cp in loads[c]:
-            cp.start()
-
     first = [
         pltpu.make_async_copy(both_hbm, both, load.at[3 * nc]),
         pltpu.make_async_copy(inv_hbm, inv, load.at[3 * nc + 1]),
     ]
+    loads = []
+    for c in range(nc):
+        cols = pl.ds(c * STEP, STEP)
+        loads.append([
+            pltpu.make_async_copy(right_hbm.at[0, cols, :], rbuf.at[0, cols, :], load.at[3 * c]),
+            pltpu.make_async_copy(right_hbm.at[1, cols, :], rbuf.at[1, cols, :], load.at[3 * c + 1]),
+            pltpu.make_async_copy(half_hbm.at[:, cols], hbuf.at[:, cols], load.at[3 * c + 2]),
+        ])
     for cp in first:
         cp.start()
-    for c in range(3):
-        fetch(c)
+    for group in loads:
+        for cp in group:
+            cp.start()
     for cp in first:
         cp.wait()
     stores = []
     for c in range(nc):
         cols = pl.ds(c * STEP, STEP)
-        if c + 3 < nc:
-            fetch(c + 3)
         for cp in loads[c]:
             cp.wait()
         rr = jnp.concatenate([rbuf[0, cols, :], rbuf[1, cols, :]], axis=1)
         bbuf[cols, :] = (rr.astype(F32) * inv[0:1, :]).astype(BF16)
         product = dot(both[...], rr, 1, 1)
         ubuf[:, cols] = product[ROWS:].astype(BF16)
-        buffer = mbuf[:, cols].astype(F32) + gbuf[:, cols].astype(F32)
-        nbuf[:, cols] = (buffer - (1.0 - MU / 100.0) * product[:ROWS]).astype(BF16)
+        nbuf[:, cols] = (hbuf[:, cols].astype(F32) - (1.0 - MU / 100.0) * product[:ROWS]).astype(BF16)
         three = [
             pltpu.make_async_copy(bbuf.at[cols, :], new_basis.at[cols, :], store.at[3 * c]),
             pltpu.make_async_copy(ubuf.at[:, cols], update.at[:, cols], store.at[3 * c + 1]),
@@ -533,16 +535,18 @@
     dma = pltpu.SemaphoreType.DMA
     zr = ROWS // NZ
     sends = 7 + 7 + 4 + 12 + 6 + 6 + 1 + 15 + 8 + 6 + 7 + 8
-    right, both, inverse = pl.pallas_call(
+    right, both, inverse, half = pl.pallas_call(
         step_kernel,
         out_shape=(
             jax.ShapeDtypeStruct((2, 2, NX, NY, BLOCK, 128), BF16),
             jax.ShapeDtypeStruct((2 * ROWS, RANK), BF16),
             jax.ShapeDtypeStruct((8, RANK), F32),
+            jax.ShapeDtypeStruct((ROWS, COLS), BF16),
         ),
         in_specs=[pl.BlockSpec(memory_space=pl.ANY)] * 3,
-        out_specs=tuple(pl.BlockSpec(memory_space=v) for v in (pl.ANY, pltpu.VMEM, pltpu.VMEM)),
+        out_specs=tuple(pl.BlockSpec(memory_space=pl.ANY) for _ in range(4)),
         scratch_shapes=[
+            pltpu.VMEM((2 * ROWS, RANK), BF16), pltpu.VMEM((8, RANK), F32),
             pltpu.VMEM((ROWS, COLS), BF16), pltpu.VMEM((ROWS, COLS), BF16), pltpu.VMEM((COLS, RANK), BF16),
             pltpu.VMEM((COLS, RANK), BF16),
             pltpu.VMEM((ROWS, RANK), BF16), pltpu.VMEM((NZ - 1, zr, RANK), BF16), pltpu.VMEM((ROWS, RANK), BF16),
@@ -554,7 +558,7 @@
             pltpu.VMEM((2, 4, BLOCK, 128), F32), pltpu.VMEM((2, 4, BLOCK, 128), BF16), pltpu.VMEM((2, 3, BLOCK, 128), BF16),
             pltpu.VMEM((8, 128), F32), pltpu.VMEM((8, 128), F32),
             pltpu.VMEM((NX * NY, 8, 128), F32), pltpu.VMEM((NZ, 8, 128), F32),
-            dma((3 * (COLS // STEP),)), dma((20,)), dma((47,)), dma((48,)), dma((16,)), dma((sends,)), dma((sends,)),
+            dma((3 * (COLS // STEP),)), dma((23,)), dma((47,)), dma((48,)), dma((16,)), dma((sends,)), dma((sends,)),
         ],
         compiler_params=pltpu.CompilerParams(collective_id=0, has_side_effects=True, vmem_limit_bytes=VMEM_LIMIT),
         name="step_kernel",
@@ -568,16 +572,16 @@
             jax.ShapeDtypeStruct((ROWS, COLS), BF16),
             jax.ShapeDtypeStruct((COLS, RANK), BF16),
         ),
-        in_specs=[pl.BlockSpec(memory_space=pl.ANY)] * 5,
+        in_specs=[pl.BlockSpec(memory_space=pl.ANY)] * 4,
         out_specs=tuple(pl.BlockSpec(memory_space=pl.ANY) for _ in range(3)),
         scratch_shapes=[
-            wide, wide, pltpu.VMEM((2 * ROWS, RANK), BF16), pltpu.VMEM((2, COLS, 128), BF16), pltpu.VMEM((8, RANK), F32),
+            wide, pltpu.VMEM((2 * ROWS, RANK), BF16), pltpu.VMEM((2, COLS, 128), BF16), pltpu.VMEM((8, RANK), F32),
             wide, wide, pltpu.VMEM((COLS, RANK), BF16),
             dma((3 * nc + 2,)), dma((3 * nc,)),
         ],
         compiler_params=pltpu.CompilerParams(vmem_limit_bytes=VMEM_LIMIT),
         name="output_kernel",
-    )(grad, momentum, both, right.reshape(2, COLS, 128), inverse)
+    )(half, both, right.reshape(2, COLS, 128), inverse)
 
 
 def solution(mesh):

time: 67.3 us -> 65.4 us (0.972)
  Pallas kernels: 66.4 us -> 64.5 us
    pallas_call x1, Pallas kernels: 5.89 us -> 4.7 us  [body(): pl.pallas_call(output_kernel, out_shape=(jax.ShapeDtypeStruct((ROWS, COLS...]
    pallas_call x1, Pallas kernels: 60.5 us -> 59.8 us  [body(): pl.pallas_call(step_kernel, out_shape=(jax.ShapeDtypeStruct((2, 2, NX, NY...]
where the time goes in v11:
time: 65.4 us; the launch traced here: 65.3 us
  Pallas kernels  64.5 us (99%)
  between operations  0.8 us (1%)
    pallas_call x1, Pallas kernels, body(): pl.pallas_call(step_kernel, out_shape=(jax.ShapeDtypeStruct((2, 2, NX, NY...  59.8 us
    pallas_call x1, Pallas kernels, body(): pl.pallas_call(output_kernel, out_shape=(jax.ShapeDtypeStruct((ROWS, COLS...  4.7 us

profile of v11, /device:TPU:1, one launch (start us, length us, event | category | flops | bytes accessed | tf_op | source)
XLA Modules:
  0.0 65.3 jit_solution(15212348725692688098)
XLA Ops:
  0.6 59.8 %step_kernel.1 = (bf16[2,2,4,4,112,128]{5,4,3,2,1,0:T(8,128)(2,1)}, bf16[512,256]{1,0:T(8,128)(2,1)}, f32[8,256]{1,0:T(8,128)}, bf16[256,3584]{1,0:T(8,128)(2,1)}) custom-call(bf16[256,3584]{1,0:T(8,128)(2,1)} %g_hbm.1, bf16[256,3584]{1,0:T(8,128)(2,1)} %m_hbm.1, bf16[3584,256]{1,0:T(8,128)(2,1)} %b_hbm.1), custom_call_target="tpu_custom_call" | custom-call | tf_op jit(solution)/shard_map/step_kernel/pallas_call | solution.py:538
  60.4 4.7 %output_kernel.1 = (bf16[256,3584]{1,0:T(8,128)(2,1)}, bf16[256,3584]{1,0:T(8,128)(2,1)}, bf16[3584,256]{1,0:T(8,128)(2,1)}) custom-call(bf16[256,3584]{1,0:T(8,128)(2,1)} %get-tuple-element.7.half_hbm, bf16[512,256]{1,0:T(8,128)(2,1)} %get-tuple-element.8.both_hbm, bf16[2,3584,128]{2,1,0:T(8,128)(2,1)} %bitcast.1, f32[8,256]{1,0:T(8,128)} %get-tuple-element.10.inv_hbm), custom_call_target="tpu_custom_call" | custom-call | tf_op jit(solution)/shard_map/output_kernel/pallas_call | solution.py:568

commit v12 on v11

--- a/solution.py
+++ b/solution.py
@@ -22,6 +22,7 @@
 COLS = N // NZ
 CHUNK = 896
 BLOCK = COLS // NF
+FAR_FIRST = sorted(range(1, NZ), key=lambda j: -min(j, NZ - j))
 STEP = 512
 VMEM_LIMIT = 60 * 1024 * 1024
 
@@ -83,10 +84,11 @@
                 det = p11 * p22 - p12 * p12
                 inv1 = reciprocal(p11)
                 mult = p12 * inv1
-                inv2 = p11 * reciprocal(det)
+                near = pl.reciprocal(det, approx=True)
+                fix = 2.0 - det * near
                 w1 = [first[a] * inv1 if a >= s else None for a in range(tiles)]
                 second = [second[a] - first[a] * mult if a >= s else None for a in range(tiles)]
-                w2 = [second[a] * inv2 if a >= s else None for a in range(tiles)]
+                w2 = [((second[a] * p11) * near) * fix if a >= s else None for a in range(tiles)]
                 if ahead is not None:
                     for k in range(s8):
                         b1, b2 = lane_of(first[s + 1], k), lane_of(second[s + 1], k)
@@ -222,26 +224,28 @@
     part[...] = (total * (1.0 / math.sqrt(N))).astype(BF16)
     ready()
     zr = ROWS // NZ
-    cps = [at.exchange(part.at[piece(at.zs[j], zr), :], rz.at[j - 1], at.zdev[j]) for j in range(1, NZ)]
+    cps = [at.exchange(part.at[piece(at.zs[j], zr), :], rz.at[j - 1], at.zdev[j]) for j in FAR_FIRST]
     for c in range(nc):
         cols = pl.ds(c * STEP, STEP)
         bht[cols, :] = gbuf[:, cols].T
     kept = pltpu.make_async_copy(gbuf, half_hbm, store.at[20])
     kept.start()
     mine = part[piece(at.t, zr), :].astype(F32)
+    for cp in cps:
+        cp.wait_recv()
     for j in range(1, NZ):
-        cps[j - 1].wait_recv()
         mine = mine + rz[j - 1].astype(F32)
     mine = mine.astype(BF16)
     left[piece(at.t, zr), :] = mine
-    az = [at.share(left.at[piece(at.t, zr), :], at.zdev[j]) for j in range(1, NZ)]
+    az = [at.share(left.at[piece(at.t, zr), :], at.zdev[j]) for j in FAR_FIRST]
 
     full = dot(mine, mine, 0, 0)
     gpart[:, 0:8, :] = full[:128, :128].reshape(16, 8, 128)
     gpart[:, 8:16, :] = full[:128, 128:].reshape(16, 8, 128)
     gpart[:, 16:24, :] = full[128:, 128:].reshape(16, 8, 128)
     owner = lax.rem(x + y, 2) == core
-    chips = [(i, j) for i in range(NX) for j in range(NY)]
+    chips = sorted(((i, j) for i in range(NX) for j in range(NY)), key=lambda c: -min(c[0], NX - c[0]) - min(c[1], NY - c[1]))
+    chips = chips[-1:] + chips[:-1]
 
     def to_owner(k, slot):
         i, j = chips[k]
@@ -283,8 +287,8 @@
             to_owner(0, slot).wait_recv()
             acc = acc + rg[slot]
         own[...] = acc
-        for cp in across:
-            cp.start()
+        for j in FAR_FIRST:
+            across[j - 1].start()
 
     for cp in az:
         cp.wait_recv()
@@ -362,19 +366,21 @@
                 total = half_of(r, h, x if h == 0 else y, k)[...] + f1[h, 3 - k].astype(F32) + f1[h, 4 + k].astype(F32)
                 sab[h, 2 * k:2 * k + 2] = total
                 s16[h, 2 * k:2 * k + 2] = total.astype(BF16)
-            for j in range(1, NX):
+            for j in (2, 1, 3):
                 if h == 0:
                     two[h].append(at.exchange(s16.at[h, ys[j]], f2.at[h, j - 1], at.dev(x, ys[j], core)))
                 else:
                     two[h].append(at.exchange(s16.at[h, xs[j]], f2.at[h, j - 1], at.dev(xs[j], y, core)))
 
-    w = lower_inverse(full, {2: second_stage})
+    unit = lax.rsqrt(full[0:1, 0:1])
+    w = lower_inverse((full * unit) * unit, {2: second_stage}) * unit
     whi, wlo = parts(w)
     halves = []
     for h in range(2):
         total = sab[h, y if h == 0 else x]
+        for cp in two[h]:
+            cp.wait_recv()
         for j in range(1, NX):
-            two[h][j - 1].wait_recv()
             total = total + f2[h, j - 1].astype(F32)
         halves.append(total)
     hi, lo = parts(jnp.concatenate(halves, axis=1))

time: 65.4 us -> 62.3 us (0.953)
  Pallas kernels: 64.5 us -> 61.4 us
    pallas_call x1, Pallas kernels: 59.8 us -> 56.7 us  [body(): pl.pallas_call(step_kernel, out_shape=(jax.ShapeDtypeStruct((2, 2, NX, NY...]
where the time goes in v12:
time: 62.3 us; the launch traced here: 62.2 us
  Pallas kernels  61.4 us (99%)
  between operations  0.8 us (1%)
    pallas_call x1, Pallas kernels, body(): pl.pallas_call(step_kernel, out_shape=(jax.ShapeDtypeStruct((2, 2, NX, NY...  56.7 us
    pallas_call x1, Pallas kernels, body(): pl.pallas_call(output_kernel, out_shape=(jax.ShapeDtypeStruct((ROWS, COLS...  4.7 us

profile of v12, /device:TPU:1, one launch (start us, length us, event | category | flops | bytes accessed | tf_op | source)
XLA Modules:
  0.0 62.2 jit_solution(15290798779231123890)
XLA Ops:
  0.6 56.7 %step_kernel.1 = (bf16[2,2,4,4,112,128]{5,4,3,2,1,0:T(8,128)(2,1)}, bf16[512,256]{1,0:T(8,128)(2,1)}, f32[8,256]{1,0:T(8,128)}, bf16[256,3584]{1,0:T(8,128)(2,1)}) custom-call(bf16[256,3584]{1,0:T(8,128)(2,1)} %g_hbm.1, bf16[256,3584]{1,0:T(8,128)(2,1)} %m_hbm.1, bf16[3584,256]{1,0:T(8,128)(2,1)} %b_hbm.1), custom_call_target="tpu_custom_call" | custom-call | tf_op jit(solution)/shard_map/step_kernel/pallas_call | solution.py:544
  57.3 4.7 %output_kernel.1 = (bf16[256,3584]{1,0:T(8,128)(2,1)}, bf16[256,3584]{1,0:T(8,128)(2,1)}, bf16[3584,256]{1,0:T(8,128)(2,1)}) custom-call(bf16[256,3584]{1,0:T(8,128)(2,1)} %get-tuple-element.7.half_hbm, bf16[512,256]{1,0:T(8,128)(2,1)} %get-tuple-element.8.both_hbm, bf16[2,3584,128]{2,1,0:T(8,128)(2,1)} %bitcast.1, f32[8,256]{1,0:T(8,128)} %get-tuple-element.10.inv_hbm), custom_call_target="tpu_custom_call" | custom-call | tf_op jit(solution)/shard_map/output_kernel/pallas_call | solution.py:574

commit v13 on v12

--- a/solution.py
+++ b/solution.py
@@ -257,12 +257,12 @@
 
     scattered = [to_owner(k, 2 * k - 1 + core if k else 0) for k in range(16)]
 
+    for k in range(1, 16):
+        scattered[k].start()
+
     @pl.when(jnp.logical_not(owner))
     def _():
         scattered[0].start()
-
-    for k in range(1, 16):
-        scattered[k].start()
 
     def to_all(k, c):
         i, j = chips[k]
@@ -315,7 +315,7 @@
             across[j - 1].wait_recv()
             acc = acc + r2[j - 1]
         gram[at.chip] = acc
-        for cp in gathered:
+        for cp in gathered[1:] + gathered[:1]:
             cp.start()
 
     for k in range(nk):
@@ -401,7 +401,7 @@
     both[0:ROWS, :] = ortho.astype(BF16)
     sc.wait_recv()
     qp[at.chip] = sq[...] + qc[...]
-    sp = [at.share(qp.at[at.chip], device) for device in at.plane]
+    sp = [at.share(qp.at[at.chip], at.dev(xs[i], ys[j], core)) for i, j in chips[1:]]
     def band(h, q, k=None, ref=out, pc=core):
         if k is None:
             return ref.at[0, pc, q] if h == 0 else ref.at[1, pc, :, q]
@@ -437,7 +437,7 @@
     for j in range(1, NX * NY):
         total = total + qp[j]
     qz[at.t] = total
-    sz = [at.share(qz.at[at.t], at.zdev[j]) for j in range(1, NZ)]
+    sz = [at.share(qz.at[at.t], at.zdev[j]) for j in FAR_FIRST]
     relays = []
     for h in range(2):
         pos, nxt, prv = at.ways[h]

time: 62.3 us -> 62.2 us (level)
  no operation moved by 1% of the time
where the time goes in v13:
time: 62.2 us; the launch traced here: 62.1 us
  Pallas kernels  61.3 us (99%)
  between operations  0.8 us (1%)
    pallas_call x1, Pallas kernels, body(): pl.pallas_call(step_kernel, out_shape=(jax.ShapeDtypeStruct((2, 2, NX, NY...  56.6 us
    pallas_call x1, Pallas kernels, body(): pl.pallas_call(output_kernel, out_shape=(jax.ShapeDtypeStruct((ROWS, COLS...  4.7 us

profile of v13, /device:TPU:1, one launch (start us, length us, event | category | flops | bytes accessed | tf_op | source)
XLA Modules:
  0.0 62.1 jit_solution(5184378689328720884)
XLA Ops:
  0.6 56.6 %step_kernel.1 = (bf16[2,2,4,4,112,128]{5,4,3,2,1,0:T(8,128)(2,1)}, bf16[512,256]{1,0:T(8,128)(2,1)}, f32[8,256]{1,0:T(8,128)}, bf16[256,3584]{1,0:T(8,128)(2,1)}) custom-call(bf16[256,3584]{1,0:T(8,128)(2,1)} %g_hbm.1, bf16[256,3584]{1,0:T(8,128)(2,1)} %m_hbm.1, bf16[3584,256]{1,0:T(8,128)(2,1)} %b_hbm.1), custom_call_target="tpu_custom_call" | custom-call | tf_op jit(solution)/shard_map/step_kernel/pallas_call | solution.py:544
  57.2 4.7 %output_kernel.1 = (bf16[256,3584]{1,0:T(8,128)(2,1)}, bf16[256,3584]{1,0:T(8,128)(2,1)}, bf16[3584,256]{1,0:T(8,128)(2,1)}) custom-call(bf16[256,3584]{1,0:T(8,128)(2,1)} %get-tuple-element.7.half_hbm, bf16[512,256]{1,0:T(8,128)(2,1)} %get-tuple-element.8.both_hbm, bf16[2,3584,128]{2,1,0:T(8,128)(2,1)} %bitcast.1, f32[8,256]{1,0:T(8,128)} %get-tuple-element.10.inv_hbm), custom_call_target="tpu_custom_call" | custom-call | tf_op jit(solution)/shard_map/output_kernel/pallas_call | solution.py:574
